TPU v7x, 128 devices: a whole 4x4x4 slice. The times are simulated.
128 devices in a mesh: dp: 2 (over x_hi), row: 8 (over x_lo, y), col: 8 (over z, core).
Axes of the slice: x: 4 (x_hi: 2, x_lo: 2; x = x_hi * 2 + x_lo), y: 4, z: 4, core: 2. Of those that a mesh axis runs over, the one named last changes fastest.
Arguments:
- inputs: bfloat16 [2, 4, 2048, 2048], P(None, 'dp', 'col', 'row'), may hold values from -6 to 6
- lengths: int32 [2, 4], P(None, 'dp'), may hold values from 512 to 2048, as said below
- ln1_gain: float32 [2048], P('row'), may hold values from 0.5 to 1.5
- ln1_bias: float32 [2048], P('row'), may hold values from -4 to 4
- w_qkv: bfloat16 [3, 2048, 2048], P(None, 'row', 'col'), may hold values from -0.125 to 0.125
- qv_bias: float32 [2, 2048], P(None, 'col'), may hold values from -4 to 4
- w_out: bfloat16 [2048, 2048], P('col', 'row'), may hold values from -0.75 to 0.75
- out_bias: float32 [2048], P('row'), may hold values from -4 to 4
- ln2_gain: float32 [2048], P('row'), may hold values from 0.5 to 1.5
- ln2_bias: float32 [2048], P('row'), may hold values from -4 to 4
- w_up: bfloat16 [2048, 8192], P('row', 'col'), may hold values from -0.125 to 0.125
- up_bias: float32 [8192], P('col'), may hold values from -4 to 4
- w_down: bfloat16 [8192, 2048], P('col', 'row'), may hold values from -0.0625 to 0.0625
- down_bias: float32 [2048], P('row'), may hold values from -4 to 4
- cotangent: bfloat16 [2, 4, 2048, 2048], P(None, 'dp', 'col', 'row'), may hold values from -6 to 6
Outputs:
- mixed: bfloat16 [2, 4, 2048, 2048], P(None, 'dp', 'col', 'row')
- input_grad: float32 [2, 4, 2048, 2048], P(None, 'dp', 'col', 'row')
- ln1_gain_grad: float32 [2048], P('row')
- ln1_bias_grad: float32 [2048], P('row')
- qkv_grad: float32 [3, 2048, 2048], P(None, 'row', 'col')
- qv_bias_grad: float32 [2, 2048], P(None, 'col')
- out_grad: float32 [2048, 2048], P('col', 'row')
- out_bias_grad: float32 [2048], P('row')
- ln2_gain_grad: float32 [2048], P('row')
- ln2_bias_grad: float32 [2048], P('row')
- up_grad: float32 [2048, 8192], P('row', 'col')
- up_bias_grad: float32 [8192], P('col')
- down_grad: float32 [8192, 2048], P('col', 'row')
- down_bias_grad: float32 [2048], P('row')
Inputs may be any that keep to these rules, and one draw needn't show every extreme that they name: `lengths`: in every micro-batch, each run of 2 sequences that one index of dp holds has one of length 2048.
All inputs are finite; a program needn't handle non-finite values.
Results may differ from a plain program's by a relative error of at most 0.035.
Values may be sent and summed in bfloat16 or wider, within the bound.
A program may use at most 256 MiB of HBM per device.

v0:
```python
import jax
import jax.numpy as jnp
from jax import lax
from jax.sharding import PartitionSpec as P

D = 2048
HEAD_DIM = 128


EPSILON = 1e-05
HUGE = 1e30


def copy_for_each(value, axis):
    peers = lax.axis_size(axis)
    return lax.all_to_all(
        jnp.broadcast_to(value[None], (peers, *value.shape)), axis, 0, 0, tiled=True
    )


def taken_together(value, axis):
    everything = copy_for_each(value, axis)
    return jnp.sum(everything, axis=0)


def packed_total(arrays, axis):
    flat, at, outs = (jnp.concatenate([a.reshape(-1) for a in arrays]), 0, [])
    total = taken_together(flat, axis)
    for a in arrays:
        outs.append(total[at : at + a.size].reshape(a.shape))
        at += a.size
    return tuple(outs)


def in_order(tiles, dim):
    tiles = jnp.moveaxis(tiles, 0, dim)
    shape = tiles.shape
    return tiles.reshape(*shape[:dim], shape[dim] * shape[dim + 1], *shape[dim + 2 :])


def gathered_copies(value, axis, dim):
    tiles = copy_for_each(value, axis)
    return in_order(tiles, dim)


def in_blocks(value, dim, peers):
    before, after = (value.shape[:dim], value.shape[dim + 1 :])
    return jnp.moveaxis(value.reshape(*before, peers, -1, *after), dim, 0)


def summed_on_arrival(value, axis, dim):
    peers = lax.axis_size(axis)
    tiles = lax.all_to_all(in_blocks(value, dim, peers), axis, 0, 0, tiled=True)
    return jnp.sum(tiles.astype(jnp.float32), axis=0)


def sent_together(arrays, axis, dim, along):
    both = jnp.concatenate(arrays, axis=along)
    whole, at, outs = (lax.all_gather(both, axis, axis=dim, tiled=True), 0, [])
    for a in arrays:
        outs.append(lax.slice_in_dim(whole, at, at + a.shape[along], axis=along))
        at += a.shape[along]
    return tuple(outs)


def of_everyone(value, axis):
    return copy_for_each(value, axis).astype(jnp.float32).sum(axis=0)


def width_totals(first, second):
    return packed_total((first, second), "row")


def col_spread(piece):
    return gathered_copies(piece, "col", 1)


def row_spread(piece):
    return lax.all_gather(piece, "row", axis=1, tiled=True)


def row_reduce(terms):
    return lax.psum_scatter(
        terms.astype(jnp.bfloat16), "row", scatter_dimension=1, tiled=True
    ).astype(jnp.float32)


def col_reduce(terms):
    return summed_on_arrival(terms.astype(jnp.bfloat16), "col", 1)


def norm_forward(values, gain, bias):
    total, squares = width_totals(jnp.sum(values, -1), jnp.sum(values * values, -1))
    middle = total / D
    spread = squares / D - middle * middle
    inverse = lax.rsqrt(spread + EPSILON)
    centred = (values - middle[..., None]) * inverse[..., None]
    return (centred, inverse, centred * gain + bias)


def norm_backward(grad, centred, inverse, gain):
    scaled = grad * gain
    total, cross = width_totals(jnp.sum(scaled, -1), jnp.sum(scaled * centred, -1))
    return inverse[..., None] * (scaled - total[..., None] / D - centred * cross[..., None] / D)


def allowed_mask(query_pos, count, seq_lengths):
    key_pos = jnp.arange(count, dtype=jnp.int32)
    allowed = (key_pos[None, None, :] <= query_pos[None, :, None]) & (
        key_pos[None, None, :] < seq_lengths[:, None, None]
    )
    return allowed[:, None]


def attend(queries, keys, values, seq_lengths, scale):
    nseq, rows, width = queries.shape
    heads = width // HEAD_DIM
    query_four = queries.reshape(nseq, rows, heads, HEAD_DIM)
    query_pos = lax.axis_index("row") * rows + jnp.arange(rows, dtype=jnp.int32)

    def fold(carry, pieces, start):
        highest, total, accum = carry
        key_piece, value_piece = pieces
        count = key_piece.shape[1]
        key_four = key_piece.reshape(nseq, count, heads, HEAD_DIM)
        value_four = value_piece.reshape(nseq, count, heads, HEAD_DIM)
        scores = (
            jnp.einsum("nqhd,nkhd->nhqk", query_four, key_four, preferred_element_type=jnp.float32)
            * scale
        )
        allowed = allowed_mask(query_pos, count, seq_lengths)
        masked = jnp.where(allowed, scores, -HUGE)
        newest = jnp.maximum(highest, jnp.max(masked, -1))
        weights = jnp.where(allowed, jnp.exp(masked - newest[..., None]), 0.0)
        total = jnp.sum(weights, -1)
        accum = jnp.einsum(
            "nhqk,nkhd->nqhd",
            weights.astype(jnp.bfloat16),
            value_four,
            preferred_element_type=jnp.float32,
        )
        return (newest, total, accum)

    start_state = (
        jnp.full((nseq, heads, rows), -HUGE, jnp.float32),
        jnp.zeros((nseq, heads, rows), jnp.float32),
        jnp.zeros((nseq, rows, heads, HEAD_DIM), jnp.float32),
    )
    highest, total, accum = fold(
        start_state, sent_together((keys, values), "row", 1, 0), jnp.int32(0)
    )
    attended = accum / jnp.transpose(total, (0, 2, 1))[..., None]
    return (attended.reshape(nseq, rows, width), highest + jnp.log(total))


def attend_back(queries, keys, values, seq_lengths, scale, logsum, grad_low, delta):
    nseq, rows, width = queries.shape
    heads = width // HEAD_DIM
    query_four = queries.reshape(nseq, rows, heads, HEAD_DIM)
    grad_four = grad_low.reshape(nseq, rows, heads, HEAD_DIM)
    query_pos = lax.axis_index("row") * rows + jnp.arange(rows, dtype=jnp.int32)
    whole = rows * lax.axis_size("row")

    def fold(carry, pieces, start):
        key_piece, value_piece = pieces
        count = key_piece.shape[1]
        key_four = key_piece.reshape(nseq, count, heads, HEAD_DIM)
        value_four = value_piece.reshape(nseq, count, heads, HEAD_DIM)
        scores = (
            jnp.einsum("nqhd,nkhd->nhqk", query_four, key_four, preferred_element_type=jnp.float32)
            * scale
        )
        allowed = allowed_mask(query_pos, count, seq_lengths)
        probs = jnp.exp(jnp.where(allowed, scores - logsum[..., None], -HUGE))
        dprob = jnp.einsum(
            "nqhd,nkhd->nhqk", grad_four, value_four, preferred_element_type=jnp.float32
        )
        dscore = (probs * (dprob - delta[..., None])).astype(jnp.bfloat16)
        dquery = (
            jnp.einsum("nhqk,nkhd->nqhd", dscore, key_four, preferred_element_type=jnp.float32)
            * scale
        )
        dkey = (
            jnp.einsum("nhqk,nqhd->nkhd", dscore, query_four, preferred_element_type=jnp.float32)
            * scale
        )
        dvalue = jnp.einsum(
            "nhqk,nqhd->nkhd",
            probs.astype(jnp.bfloat16),
            grad_four,
            preferred_element_type=jnp.float32,
        )
        block = jnp.concatenate(
            [dkey.reshape(nseq, count, width), dvalue.reshape(nseq, count, width)], -1
        )
        return (dquery, block)

    start_state = (
        jnp.zeros((nseq, rows, heads, HEAD_DIM), jnp.float32),
        jnp.zeros((nseq, whole, 2 * width), jnp.float32),
    )
    dquery, dpairs = fold(start_state, sent_together((keys, values), "row", 1, 0), jnp.int32(0))
    return (dquery.reshape(nseq, rows, width), dpairs)


def shards(
    inputs,
    lengths,
    ln1_gain,
    ln1_bias,
    w_qkv,
    qv_bias,
    w_out,
    out_bias,
    ln2_gain,
    ln2_bias,
    w_up,
    up_bias,
    w_down,
    down_bias,
    cotangent,
):
    scale = HEAD_DIM ** (-0.5)
    grad_qkv = jnp.zeros(w_qkv.shape, jnp.float32)
    grad_qv_bias = jnp.zeros(qv_bias.shape, jnp.float32)
    grad_out = jnp.zeros(w_out.shape, jnp.float32)
    grad_out_bias = jnp.zeros(out_bias.shape, jnp.float32)
    grad_up = jnp.zeros(w_up.shape, jnp.float32)
    grad_up_bias = jnp.zeros(up_bias.shape, jnp.float32)
    grad_down = jnp.zeros(w_down.shape, jnp.float32)
    grad_down_bias = jnp.zeros(down_bias.shape, jnp.float32)
    gain_one = jnp.zeros(ln1_gain.shape, jnp.float32)
    shift_one = jnp.zeros(ln1_gain.shape, jnp.float32)
    gain_two = jnp.zeros(ln1_gain.shape, jnp.float32)
    shift_two = jnp.zeros(ln1_gain.shape, jnp.float32)
    results = []
    input_grads = []
    for micro in range(inputs.shape[0]):
        tokens = inputs[micro].astype(jnp.float32)
        seq_lengths = lengths[micro]
        centred_one, inverse_one, normed_one = norm_forward(tokens, ln1_gain, ln1_bias)
        low_one = normed_one.astype(jnp.bfloat16)
        spread_one = col_spread(low_one)
        nseq, whole, _ = spread_one.shape
        width = w_qkv.shape[2]
        partial_value = jnp.einsum(
            "nsd,jdc->nsjc", spread_one, w_qkv, preferred_element_type=jnp.float32
        )
        projected = row_reduce(partial_value.reshape(nseq, whole, 3 * width))
        queries = (projected[..., :width] + qv_bias[0]).astype(jnp.bfloat16)
        keys = projected[..., width : 2 * width].astype(jnp.bfloat16)
        values = (projected[..., 2 * width :] + qv_bias[1]).astype(jnp.bfloat16)
        attended, logsum = attend(queries, keys, values, seq_lengths, scale)
        att_low = attended.astype(jnp.bfloat16)
        spread_att = row_spread(att_low)
        branch = (
            col_reduce(
                jnp.einsum("nsc,cd->nsd", spread_att, w_out, preferred_element_type=jnp.float32)
            )
            + out_bias
        )
        middle = tokens + branch
        centred_two, inverse_two, normed_two = norm_forward(middle, ln2_gain, ln2_bias)
        low_two = normed_two.astype(jnp.bfloat16)
        spread_two = col_spread(low_two)
        own_two = lax.all_to_all(spread_two, "row", split_axis=1, concat_axis=2, tiled=True)
        hidden = (
            jnp.einsum(
                "nsd,df->nsf",
                own_two,
                lax.all_gather(w_up, "row", axis=0, tiled=True),
                preferred_element_type=jnp.float32,
            )
            + up_bias
        )
        act_low = jax.nn.gelu(hidden, approximate=False).astype(jnp.bfloat16)
        spread_act = row_spread(act_low)
        second = (
            col_reduce(
                jnp.einsum("nsf,fd->nsd", spread_act, w_down, preferred_element_type=jnp.float32)
            )
            + down_bias
        )
        results.append((middle + second).astype(jnp.bfloat16))
        upstream = cotangent[micro].astype(jnp.float32)
        spread_dsecond = col_spread(upstream.astype(jnp.bfloat16))
        grad_down = grad_down + jnp.einsum(
            "nsf,nsd->fd", spread_act, spread_dsecond, preferred_element_type=jnp.float32
        )
        grad_down_bias = grad_down_bias + jnp.sum(spread_dsecond.astype(jnp.float32), (0, 1))
        own_dsecond = lax.all_to_all(spread_dsecond, "row", split_axis=1, concat_axis=2, tiled=True)
        dactivation = jnp.einsum(
            "nsd,fd->nsf",
            own_dsecond,
            lax.all_gather(w_down, "row", axis=1, tiled=True),
            preferred_element_type=jnp.float32,
        )
        gelu_value, gelu_pull = jax.vjp(lambda inner: jax.nn.gelu(inner, approximate=False), hidden)
        dhidden = gelu_pull(dactivation)[0].astype(jnp.bfloat16)
        spread_dhidden = row_spread(dhidden)
        grad_up = grad_up + jnp.einsum(
            "nsd,nsf->df", spread_two, spread_dhidden, preferred_element_type=jnp.float32
        )
        grad_up_bias = grad_up_bias + jnp.sum(spread_dhidden.astype(jnp.float32), (0, 1))
        dnormed_two = col_reduce(
            jnp.einsum("nsf,df->nsd", spread_dhidden, w_up, preferred_element_type=jnp.float32)
        )
        gain_two = gain_two + jnp.sum(dnormed_two * centred_two, (0, 1))
        shift_two = shift_two + jnp.sum(dnormed_two, (0, 1))
        dmiddle = upstream + norm_backward(dnormed_two, centred_two, inverse_two, ln2_gain)
        spread_dbranch = col_spread(dmiddle.astype(jnp.bfloat16))
        grad_out = grad_out + jnp.einsum(
            "nsc,nsd->cd", spread_att, spread_dbranch, preferred_element_type=jnp.float32
        )
        grad_out_bias = grad_out_bias + jnp.sum(spread_dbranch.astype(jnp.float32), (0, 1))
        dattended = row_reduce(
            jnp.einsum("nsd,cd->nsc", spread_dbranch, w_out, preferred_element_type=jnp.float32)
        ).astype(jnp.bfloat16)
        rows = queries.shape[1]
        heads = width // HEAD_DIM
        grad_four = dattended.reshape(nseq, rows, heads, HEAD_DIM).astype(jnp.float32)
        delta = jnp.transpose(
            jnp.sum(grad_four * attended.reshape(nseq, rows, heads, HEAD_DIM), -1), (0, 2, 1)
        )
        dquery, dpairs = attend_back(
            queries, keys, values, seq_lengths, scale, logsum, dattended, delta
        )
        dpairs_own = row_reduce(dpairs)
        dprojected = jnp.concatenate([dquery, dpairs_own], -1).astype(jnp.bfloat16)
        spread_dprojected = row_spread(dprojected).reshape(nseq, whole, 3, width)
        grad_qkv = grad_qkv + jnp.einsum(
            "nsd,nsjc->jdc", spread_one, spread_dprojected, preferred_element_type=jnp.float32
        )
        bias_terms = jnp.sum(spread_dprojected.astype(jnp.float32), (0, 1))
        grad_qv_bias = grad_qv_bias + jnp.stack([bias_terms[0], bias_terms[2]])
        dnormed_one = col_reduce(
            jnp.einsum(
                "nsjc,jdc->nsd", spread_dprojected, w_qkv, preferred_element_type=jnp.float32
            )
        )
        gain_one = gain_one + jnp.sum(dnormed_one * centred_one, (0, 1))
        shift_one = shift_one + jnp.sum(dnormed_one, (0, 1))
        input_grads.append(dmiddle + norm_backward(dnormed_one, centred_one, inverse_one, ln1_gain))
    summed = (
        of_everyone(grad_qkv.astype(jnp.bfloat16), "dp").astype(jnp.float32),
        of_everyone(grad_qv_bias.astype(jnp.bfloat16), "dp").astype(jnp.float32),
        of_everyone(grad_out.astype(jnp.bfloat16), "dp").astype(jnp.float32),
        of_everyone(grad_out_bias.astype(jnp.bfloat16), "dp").astype(jnp.float32),
        of_everyone(grad_up.astype(jnp.bfloat16), "dp").astype(jnp.float32),
        of_everyone(grad_up_bias.astype(jnp.bfloat16), "dp").astype(jnp.float32),
        of_everyone(grad_down.astype(jnp.bfloat16), "dp").astype(jnp.float32),
        of_everyone(grad_down_bias.astype(jnp.bfloat16), "dp").astype(jnp.float32),
    )
    norms = packed_total((gain_one, shift_one, gain_two, shift_two), ("dp", "col"))
    return (
        jnp.stack(results),
        jnp.stack(input_grads),
        norms[0],
        norms[1],
        summed[0],
        summed[1],
        summed[2],
        summed[3],
        norms[2],
        norms[3],
        summed[4],
        summed[5],
        summed[6],
        summed[7],
    )


def solution(mesh):
    in_specs = (
        P(None, "dp", "col", "row"),
        P(None, "dp"),
        P("row"),
        P("row"),
        P(None, "row", "col"),
        P(None, "col"),
        P("col", "row"),
        P("row"),
        P("row"),
        P("row"),
        P("row", "col"),
        P("col"),
        P("col", "row"),
        P("row"),
        P(None, "dp", "col", "row"),
    )
    out_specs = (
        P(None, "dp", "col", "row"),
        P(None, "dp", "col", "row"),
        P("row"),
        P("row"),
        P(None, "row", "col"),
        P(None, "col"),
        P("col", "row"),
        P("row"),
        P("row"),
        P("row"),
        P("row", "col"),
        P("col"),
        P("col", "row"),
        P("row"),
    )
    return jax.shard_map(shards, mesh=mesh, in_specs=in_specs, out_specs=out_specs, check_vma=False)
```

profile of v0, /device:TPU:1, one launch (start us, length us, event | category | flops | bytes accessed | tf_op | source)
XLA Modules:
  0.0 1764.8 jit_solution(1792670289022624030)
XLA Ops:
  42.4 26.3 %all-to-all-done.1 = bf16[8,2,256,256]{3,2,1,0:T(8,128)(2,1)} async-done(((bf16[8,2,256,256]{3,2,1,0:T(8,128)(2,1)}), bf16[8,2,256,256]{3,2,1,0:T(8,128)(2,1)}, u32[]{:S(2)}, u32[]{:S(2)}) %all-to-all-start.1) | async-done | bytes 2097184 | tf_op jit(solution)/shard_map/all_to_all | solution.py:16
  76.5 30.2 %all_to_all.249 = bf16[8,2,256,256]{3,2,1,0:T(8,128)(2,1)S(1)} all-to-all(bf16[8,2,256,256]{3,2,1,0:T(8,128)(2,1)S(1)} %broadcast_in_dim.113), channel_id=1, replica_groups=mesh['dp'=2,'row'=8,'col'=8] {'col'}, dimensions={0} | all-to-all | bytes 4194304 | tf_op jit(solution)/shard_map/all_to_all | solution.py:16
  113.4 33.3 %reduce-scatter.7.cloned.1.call-done = bf16[2,256,768]{2,1,0:T(8,128)(2,1)} async-done(((bf16[2,2048,768]{2,1,0:T(8,128)(2,1)}), bf16[2,256,768]{2,1,0:T(8,128)(2,1)}) %reduce-scatter.7.cloned.1.call-update) | async-done | bytes 786448 | tf_op jit(solution)/shard_map/reduce_scatter | solution.py:83
  148.0 72.9 %reduce-scatter.9.cloned.1.call-done = bf16[2,256,768]{2,1,0:T(8,128)(2,1)} async-done(((bf16[2,2048,768]{2,1,0:T(8,128)(2,1)}), bf16[2,256,768]{2,1,0:T(8,128)(2,1)}) %reduce-scatter.9.cloned.1.call-update) | async-done | bytes 786448 | tf_op jit(solution)/shard_map/reduce_scatter | solution.py:83
  227.0 48.4 %all-gather.21.cloned.1.call-done = bf16[4,2048,256]{2,1,0:T(8,128)(2,1)} async-done(((bf16[4,256,256]{2,1,0:T(8,128)(2,1)}), bf16[4,2048,256]{2,1,0:T(8,128)(2,1)}) %all-gather.21.cloned.1.call-update) | async-done | bytes 4194320 | tf_op jit(solution)/shard_map/all_gather | solution.py:59
  296.2 32.7 %all-gather.13.cloned.1.call-done = bf16[4,2048,256]{2,1,0:T(8,128)(2,1)} async-done(((bf16[4,256,256]{2,1,0:T(8,128)(2,1)}), bf16[4,2048,256]{2,1,0:T(8,128)(2,1)}) %all-gather.13.cloned.1.call-update) | async-done | bytes 4194320 | tf_op jit(solution)/shard_map/all_gather | solution.py:59
  349.3 16.5 all-gather.23.cloned.1.call-done
  380.4 28.6 %all-gather.15.cloned.1.call-done = bf16[2,2048,256]{2,1,0:T(8,128)(2,1)} async-done(((bf16[2,256,256]{2,1,0:T(8,128)(2,1)}), bf16[2,2048,256]{2,1,0:T(8,128)(2,1)}) %all-gather.15.cloned.1.call-update) | async-done | bytes 2097168 | tf_op jit(solution)/shard_map/all_gather | solution.py:79
  424.1 25.7 %all-to-all-done.2 = bf16[8,2,256,256]{3,2,1,0:T(8,128)(2,1)} async-done(((bf16[8,2,256,256]{3,2,1,0:T(8,128)(2,1)}), bf16[8,2,256,256]{3,2,1,0:T(8,128)(2,1)}, u32[]{:S(2)}, u32[]{:S(2)}) %all-to-all-start.2) | async-done | bytes 2097184 | tf_op jit(solution)/shard_map/all_to_all | solution.py:53
  461.6 21.3 %all-to-all-done.14 = bf16[8,2,256,256]{3,2,1,0:T(8,128)(2,1)} async-done(((bf16[8,2,256,256]{3,2,1,0:T(8,128)(2,1)}), bf16[8,2,256,256]{3,2,1,0:T(8,128)(2,1)}, u32[]{:S(2)}, u32[]{:S(2)}) %all-to-all-start.14) | async-done | bytes 2097184 | tf_op jit(solution)/shard_map/all_to_all | solution.py:16
  499.7 14.0 copy.290
  521.2 23.9 %all-to-all-done.15 = bf16[2,2048,256]{2,0,1:T(2,128)(2,1)} async-done(((bf16[2,2048,256]{2,0,1:T(2,128)(2,1)}), bf16[2,2048,256]{2,0,1:T(2,128)(2,1)}, u32[]{:S(2)}, u32[]{:S(2)}) %all-to-all-start.15) | async-done | bytes 2097184 | tf_op jit(solution)/shard_map/all_to_all | solution.py:291
  551.9 26.3 %all-to-all-done.4 = bf16[8,2,256,256]{2,3,1,0:T(8,128)(2,1)} async-done(((bf16[8,2,256,256]{2,3,1,0:T(8,128)(2,1)}), bf16[8,2,256,256]{2,3,1,0:T(8,128)(2,1)}, u32[]{:S(2)}, u32[]{:S(2)}) %all-to-all-start.4) | async-done | bytes 2097184 | tf_op jit(solution)/shard_map/all_to_all | solution.py:16
  594.3 17.0 all-to-all-done.11
  625.8 21.7 %all-to-all-done.5 = bf16[2,2048,256]{2,0,1:T(2,128)(2,1)} async-done(((bf16[2,2048,256]{2,0,1:T(2,128)(2,1)}), bf16[2,2048,256]{2,0,1:T(2,128)(2,1)}, u32[]{:S(2)}, u32[]{:S(2)}) %all-to-all-start.5) | async-done | bytes 2097184 | tf_op jit(solution)/shard_map/all_to_all | solution.py:266
  669.4 17.6 all-to-all-done.12
  722.9 35.1 %all_to_all.250 = bf16[8,2,256,256]{3,2,1,0:T(8,128)(2,1)S(1)} all-to-all(bf16[8,2,256,256]{3,2,1,0:T(8,128)(2,1)S(1)} %broadcast_in_dim.125), channel_id=1, replica_groups=mesh['dp'=2,'row'=8,'col'=8] {'col'}, dimensions={0} | all-to-all | bytes 4194304 | tf_op jit(solution)/shard_map/all_to_all | solution.py:16
  759.3 12.7 copy.304
  772.1 52.5 %all_to_all.251 = bf16[2,2048,256]{2,0,1:T(2,128)(2,1)S(1)} all-to-all(bf16[2,2048,256]{2,0,1:T(2,128)(2,1)S(1)} %copy.304), channel_id=1, replica_groups=mesh['dp'=2,'row'=8,'col'=8] {'row'}, dimensions={1} | all-to-all | bytes 4194304 | tf_op jit(solution)/shard_map/all_to_all | solution.py:291
  851.6 78.6 %all-gather.33.cloned.1.call-done = bf16[2,2048,1024]{2,1,0:T(8,128)(2,1)} async-done(((bf16[2,256,1024]{2,1,0:T(8,128)(2,1)}), bf16[2,2048,1024]{2,1,0:T(8,128)(2,1)}) %all-gather.33.cloned.1.call-update) | async-done | bytes 8388624 | tf_op jit(solution)/shard_map/all_gather | solution.py:79
  946.1 23.2 %all-to-all-done.23 = bf16[8,2,256,256]{3,2,1,0:T(8,128)(2,1)} async-done(((bf16[8,2,256,256]{3,2,1,0:T(8,128)(2,1)}), bf16[8,2,256,256]{3,2,1,0:T(8,128)(2,1)}, u32[]{:S(2)}, u32[]{:S(2)}) %all-to-all-start.23) | async-done | bytes 2097184 | tf_op jit(solution)/shard_map/all_to_all | solution.py:53
  1005.0 31.9 %all_to_all.252 = bf16[8,2,256,256]{3,2,1,0:T(8,128)(2,1)S(1)} all-to-all(bf16[8,2,256,256]{3,2,1,0:T(8,128)(2,1)S(1)} %broadcast_in_dim.122), channel_id=1, replica_groups=mesh['dp'=2,'row'=8,'col'=8] {'col'}, dimensions={0} | all-to-all | bytes 4194304 | tf_op jit(solution)/shard_map/all_to_all | solution.py:16
  1042.8 30.0 %all_to_all.253 = bf16[8,2,256,256]{3,2,1,0:T(8,128)(2,1)S(1)} all-to-all(bf16[8,2,256,256]{3,2,1,0:T(8,128)(2,1)S(1)} %broadcast_in_dim.128), channel_id=1, replica_groups=mesh['dp'=2,'row'=8,'col'=8] {'col'}, dimensions={0} | all-to-all | bytes 4194304 | tf_op jit(solution)/shard_map/all_to_all | solution.py:16
  1098.3 23.4 %reduce-scatter.15.cloned.1.call-done = bf16[2,256,256]{2,1,0:T(8,128)(2,1)} async-done(((bf16[2,2048,256]{2,1,0:T(8,128)(2,1)}), bf16[2,256,256]{2,1,0:T(8,128)(2,1)}) %reduce-scatter.15.cloned.1.call-update) | async-done | bytes 262160 | tf_op jit(solution)/shard_map/reduce_scatter | solution.py:83
  1145.5 35.8 %reduce-scatter.13.cloned.1.call-done = bf16[2,256,512]{1,2,0:T(8,128)(2,1)} async-done(((bf16[2,2048,512]{1,2,0:T(8,128)(2,1)}), bf16[2,256,512]{1,2,0:T(8,128)(2,1)}) %reduce-scatter.13.cloned.1.call-update) | async-done | bytes 524304 | tf_op jit(solution)/shard_map/reduce_scatter | solution.py:83
  1187.6 47.7 %reduce-scatter.17.cloned.1.call-done = bf16[2,256,512]{1,2,0:T(8,128)(2,1)} async-done(((bf16[2,2048,512]{1,2,0:T(8,128)(2,1)}), bf16[2,256,512]{1,2,0:T(8,128)(2,1)}) %reduce-scatter.17.cloned.1.call-update) | async-done | bytes 524304 | tf_op jit(solution)/shard_map/reduce_scatter | solution.py:83
  1259.9 68.3 %all-gather.25.cloned.1.call-done = bf16[2,2048,1024]{2,1,0:T(8,128)(2,1)} async-done(((bf16[2,256,1024]{2,1,0:T(8,128)(2,1)}), bf16[2,2048,1024]{2,1,0:T(8,128)(2,1)}) %all-gather.25.cloned.1.call-update) | async-done | bytes 8388624 | tf_op jit(solution)/shard_map/all_gather | solution.py:79
  1352.1 80.2 %all-gather.19.cloned.1.call-done = bf16[2,2048,1024]{2,1,0:T(8,128)(2,1)} async-done(((bf16[2,256,1024]{2,1,0:T(8,128)(2,1)}), bf16[2,2048,1024]{2,1,0:T(8,128)(2,1)}) %all-gather.19.cloned.1.call-update) | async-done | bytes 8388624 | tf_op jit(solution)/shard_map/all_gather | solution.py:79
  1481.3 15.2 all-to-all-done.13
  1505.9 15.0 all-gather.31.cloned.1.call-done
  1524.5 74.9 %all-gather.35.cloned.1.call-done = bf16[2,2048,768]{1,2,0:T(8,128)(2,1)} async-done(((bf16[2,256,768]{1,2,0:T(8,128)(2,1)}), bf16[2,2048,768]{1,2,0:T(8,128)(2,1)}) %all-gather.35.cloned.1.call-update) | async-done | bytes 6291472 | tf_op jit(solution)/shard_map/all_gather | solution.py:79
  1669.2 19.1 %all-to-all-done.19 = bf16[8,2,256,256]{3,2,1,0:T(8,128)(2,1)} async-done(((bf16[8,2,256,256]{3,2,1,0:T(8,128)(2,1)}), bf16[8,2,256,256]{3,2,1,0:T(8,128)(2,1)}, u32[]{:S(2)}, u32[]{:S(2)}) %all-to-all-start.19) | async-done | bytes 2097184 | tf_op jit(solution)/shard_map/all_to_all | solution.py:53
  (487 shorter events, 648.8 us)
Async XLA Ops:
  33.5 35.1 %all-to-all-start.1 = ((bf16[8,2,256,256]{3,2,1,0:T(8,128)(2,1)}), bf16[8,2,256,256]{3,2,1,0:T(8,128)(2,1)}, u32[]{:S(2)}, u32[]{:S(2)}) async-start(bf16[8,2,256,256]{3,2,1,0:T(8,128)(2,1)} %broadcast_in_dim.104), calls=%async_computation.1 | async-start | bytes 4194304 | tf_op jit(solution)/shard_map/all_to_all | solution.py:16
  42.3 104.5 %reduce-scatter.7.cloned.1.call-start = ((), (), s32[]{:S(2)}) async-start(), calls=%async_computation.43 | async-start | bytes 7077888 | tf_op jit(solution)/shard_map/reduce_scatter | solution.py:83
  76.3 144.6 %reduce-scatter.9.cloned.1.call-start = ((), (), s32[]{:S(2)}) async-start(), calls=%async_computation.48 | async-start | bytes 7077888 | tf_op jit(solution)/shard_map/reduce_scatter | solution.py:83
  112.8 162.6 %all-gather.21.cloned.1.call-start = ((), (), s32[]{:S(2)}) async-start(), calls=%async_computation.49 | async-start | bytes 4718592 | tf_op jit(solution)/shard_map/all_gather | solution.py:59
  223.9 105.0 %all-gather.13.cloned.1.call-start = ((), (), s32[]{:S(2)}) async-start(), calls=%async_computation.44 | async-start | bytes 4718592 | tf_op jit(solution)/shard_map/all_gather | solution.py:59
  224.8 140.9 %all-gather.23.cloned.1.call-start = ((), (), s32[]{:S(2)}) async-start(), calls=%async_computation.50 | async-start | bytes 2359296 | tf_op jit(solution)/shard_map/all_gather | solution.py:79
  295.8 113.2 %all-gather.15.cloned.1.call-start = ((), (), s32[]{:S(2)}) async-start(), calls=%async_computation.45 | async-start | bytes 2359296 | tf_op jit(solution)/shard_map/all_gather | solution.py:79
  369.5 43.2 %all-to-all-start.9 = ((bf16[8,2,256,256]{3,2,1,0:T(8,128)(2,1)}), bf16[8,2,256,256]{3,2,1,0:T(8,128)(2,1)}, u32[]{:S(2)}, u32[]{:S(2)}) async-start(bf16[8,2,256,256]{3,2,1,0:T(8,128)(2,1)} %bitcast.500), calls=%async_computation.11 | async-start | bytes 4194304 | tf_op jit(solution)/shard_map/all_to_all | solution.py:53
  412.7 37.1 %all-to-all-start.2 = ((bf16[8,2,256,256]{3,2,1,0:T(8,128)(2,1)}), bf16[8,2,256,256]{3,2,1,0:T(8,128)(2,1)}, u32[]{:S(2)}, u32[]{:S(2)}) async-start(bf16[8,2,256,256]{3,2,1,0:T(8,128)(2,1)} %bitcast.499), calls=%async_computation.3 | async-start | bytes 4194304 | tf_op jit(solution)/shard_map/all_to_all | solution.py:53
  456.4 238.9 %all-gather.17.cloned.1.call-start = ((), (), s32[]{:S(2)}) async-start(), calls=%async_computation.46 | async-start | bytes 4718592 | tf_op jit(solution)/shard_map/all_gather | solution.py:271
  579.7 31.6 %all-to-all-start.11 = ((bf16[8,2,256,256]{2,3,1,0:T(8,128)(2,1)}), bf16[8,2,256,256]{2,3,1,0:T(8,128)(2,1)}, u32[]{:S(2)}, u32[]{:S(2)}) async-start(bf16[8,2,256,256]{2,3,1,0:T(8,128)(2,1)} %broadcast_in_dim.117), calls=%async_computation.13 | async-start | bytes 4194304 | tf_op jit(solution)/shard_map/all_to_all | solution.py:16
  611.3 36.1 %all-to-all-start.5 = ((bf16[2,2048,256]{2,0,1:T(2,128)(2,1)}), bf16[2,2048,256]{2,0,1:T(2,128)(2,1)}, u32[]{:S(2)}, u32[]{:S(2)}) async-start(bf16[2,2048,256]{2,0,1:T(2,128)(2,1)} %copy.273), calls=%async_computation.6 | async-start | bytes 4194304 | tf_op jit(solution)/shard_map/all_to_all | solution.py:266
  615.7 98.9 %all-gather.27.cloned.1.call-start = ((), (), s32[]{:S(2)}) async-start(), calls=%async_computation.52 | async-start | bytes 4718592 | tf_op jit(solution)/shard_map/all_gather | solution.py:295
  647.5 39.6 %all-to-all-start.12 = ((bf16[2,2048,256]{2,0,1:T(2,128)(2,1)}), bf16[2,2048,256]{2,0,1:T(2,128)(2,1)}, u32[]{:S(2)}, u32[]{:S(2)}) async-start(bf16[2,2048,256]{2,0,1:T(2,128)(2,1)} %copy.286), calls=%async_computation.14 | async-start | bytes 4194304 | tf_op jit(solution)/shard_map/all_to_all | solution.py:266
  652.3 187.2 %all-gather.29.cloned.1.call-start = ((), (), s32[]{:S(2)}) async-start(), calls=%async_computation.53 | async-start | bytes 9437184 | tf_op jit(solution)/shard_map/all_gather | solution.py:79
  722.7 207.5 %all-gather.33.cloned.1.call-start = ((), (), s32[]{:S(2)}) async-start(), calls=%async_computation.57 | async-start | bytes 9437184 | tf_op jit(solution)/shard_map/all_gather | solution.py:79
  846.7 90.7 %all-to-all-start.16 = ((bf16[8,2,256,256]{3,2,1,0:T(8,128)(2,1)}), bf16[8,2,256,256]{3,2,1,0:T(8,128)(2,1)}, u32[]{:S(2)}, u32[]{:S(2)}) async-start(bf16[8,2,256,256]{3,2,1,0:T(8,128)(2,1)} %bitcast.501), calls=%async_computation.18 | async-start | bytes 4194304 | tf_op jit(solution)/shard_map/all_to_all | solution.py:53
  937.4 31.8 %all-to-all-start.23 = ((bf16[8,2,256,256]{3,2,1,0:T(8,128)(2,1)}), bf16[8,2,256,256]{3,2,1,0:T(8,128)(2,1)}, u32[]{:S(2)}, u32[]{:S(2)}) async-start(bf16[8,2,256,256]{3,2,1,0:T(8,128)(2,1)} %bitcast.498), calls=%async_computation.27 | async-start | bytes 4194304 | tf_op jit(solution)/shard_map/all_to_all | solution.py:53
  991.5 86.9 %reduce-scatter.11.cloned.1.call-start = ((), (), s32[]{:S(2)}) async-start(), calls=%async_computation.54 | async-start | bytes 2359296 | tf_op jit(solution)/shard_map/reduce_scatter | solution.py:83
  1041.7 80.0 %reduce-scatter.15.cloned.1.call-start = ((), (), s32[]{:S(2)}) async-start(), calls=%async_computation.58 | async-start | bytes 2359296 | tf_op jit(solution)/shard_map/reduce_scatter | solution.py:83
  1077.6 103.6 %reduce-scatter.13.cloned.1.call-start = ((), (), s32[]{:S(2)}) async-start(), calls=%async_computation.55 | async-start | bytes 4718592 | tf_op jit(solution)/shard_map/reduce_scatter | solution.py:83
  1097.6 137.7 %reduce-scatter.17.cloned.1.call-start = ((), (), s32[]{:S(2)}) async-start(), calls=%async_computation.59 | async-start | bytes 4718592 | tf_op jit(solution)/shard_map/reduce_scatter | solution.py:83
  1139.9 188.3 %all-gather.25.cloned.1.call-start = ((), (), s32[]{:S(2)}) async-start(), calls=%async_computation.51 | async-start | bytes 9437184 | tf_op jit(solution)/shard_map/all_gather | solution.py:79
  1140.5 291.8 %all-gather.19.cloned.1.call-start = ((), (), s32[]{:S(2)}) async-start(), calls=%async_computation.47 | async-start | bytes 9437184 | tf_op jit(solution)/shard_map/all_gather | solution.py:79
  1141.0 379.8 %all-gather.31.cloned.1.call-start = ((), (), s32[]{:S(2)}) async-start(), calls=%async_computation.56 | async-start | bytes 7077888 | tf_op jit(solution)/shard_map/all_gather | solution.py:79
  1183.2 416.3 %all-gather.35.cloned.1.call-start = ((), (), s32[]{:S(2)}) async-start(), calls=%async_computation.60 | async-start | bytes 7077888 | tf_op jit(solution)/shard_map/all_gather | solution.py:79
  1243.5 93.3 %all-to-all-start.36 = ((bf16[2,2,128]{2,1,0:T(2,128)(2,1)}), bf16[2,2,128]{2,1,0:T(2,128)(2,1)S(1)}, u32[]{:S(2)}, u32[]{:S(2)}) async-start(bf16[2,2,128]{2,1,0:T(2,128)(2,1)} %reshape.774), calls=%async_computation.42 | async-start | bytes 2048 | tf_op jit(solution)/shard_map/all_to_all | solution.py:16
  1347.9 91.0 %all-to-all-start.33 = ((bf16[2,256,1024]{2,1,0:T(8,128)(2,1)}), bf16[2,256,1024]{2,1,0:T(8,128)(2,1)S(1)}, u32[]{:S(2)}, u32[]{:S(2)}) async-start(bf16[2,256,1024]{2,1,0:T(8,128)(2,1)} %broadcast_in_dim.135), calls=%async_computation.39 | async-start | bytes 2097152 | tf_op jit(solution)/shard_map/all_to_all | solution.py:16
  1464.5 32.1 %all-to-all-start.13 = ((bf16[8,2,256,256]{3,2,1,0:T(8,128)(2,1)}), bf16[8,2,256,256]{3,2,1,0:T(8,128)(2,1)}, u32[]{:S(2)}, u32[]{:S(2)}) async-start(bf16[8,2,256,256]{3,2,1,0:T(8,128)(2,1)} %bitcast.497), calls=%async_computation.15 | async-start | bytes 4194304 | tf_op jit(solution)/shard_map/all_to_all | solution.py:53
  1496.5 112.3 %all-to-all-start.6 = ((bf16[8,2,256,256]{3,2,1,0:T(8,128)(2,1)}), bf16[8,2,256,256]{3,2,1,0:T(8,128)(2,1)}, u32[]{:S(2)}, u32[]{:S(2)}) async-start(bf16[8,2,256,256]{3,2,1,0:T(8,128)(2,1)} %bitcast.495), calls=%async_computation.7 | async-start | bytes 4194304 | tf_op jit(solution)/shard_map/all_to_all | solution.py:53
  1649.4 38.8 %all-to-all-start.19 = ((bf16[8,2,256,256]{3,2,1,0:T(8,128)(2,1)}), bf16[8,2,256,256]{3,2,1,0:T(8,128)(2,1)}, u32[]{:S(2)}, u32[]{:S(2)}) async-start(bf16[8,2,256,256]{3,2,1,0:T(8,128)(2,1)} %bitcast.496), calls=%async_computation.23 | async-start | bytes 4194304 | tf_op jit(solution)/shard_map/all_to_all | solution.py:53
  1688.2 31.6 %all-to-all-start.26 = ((bf16[8,2,256,256]{3,2,1,0:T(8,128)(2,1)}), bf16[8,2,256,256]{3,2,1,0:T(8,128)(2,1)}, u32[]{:S(2)}, u32[]{:S(2)}) async-start(bf16[8,2,256,256]{3,2,1,0:T(8,128)(2,1)} %bitcast.494), calls=%async_computation.32 | async-start | bytes 4194304 | tf_op jit(solution)/shard_map/all_to_all | solution.py:53
  (93 other events, 1204.8 us)
Sparse Core Ops, SparseCore 0:
  76.4 70.2 reduce-scatter.6
  149.1 71.6 reduce-scatter.8
  224.0 51.3 all-gather.20
  277.5 51.3 all-gather.12
  331.0 34.7 all-gather.22
  367.8 41.0 all-gather.14
  458.9 52.0 all-gather.16
  618.1 95.1 all-gather.26
  722.8 115.3 all-gather.28
  839.6 90.4 all-gather.32
  1041.8 36.4 reduce-scatter.10
  1080.6 41.0 reduce-scatter.14
  1124.1 57.0 reduce-scatter.12
  1183.5 51.8 reduce-scatter.16
  1237.4 90.6 all-gather.24
  1330.2 102.0 all-gather.18
  1434.3 86.5 all-gather.30
  1522.3 77.1 all-gather.34
where the time goes:
time: 1770 us; the launch traced here: 1760 us
  waiting for transfers between devices  967 us (55%)
  blocking collectives  180 us (10%)
  matrix products  171 us (10%)
  starting transfers between devices  170 us (10%)
  local copies, waits for them, and re-layouts  166 us (9%)
  other arithmetic  94.7 us (5%)
    all_gather x8, waiting for transfers between devices, row_spread(): return lax.all_gather(piece, 'row', axis=1, tiled=True)  362 us
    reduce_scatter x6, waiting for transfers between devices, row_reduce(): lax.psum_scatter(terms.astype(jnp.bfloat16), 'row', scatter_dimension=1,...  213 us
    all_to_all x21, waiting for transfers between devices, copy_for_each(): lax.all_to_all(jnp.broadcast_to(value[None], (peers, *value.shape)), axis...  150 us
    all_to_all x4, blocking collectives, copy_for_each(): lax.all_to_all(jnp.broadcast_to(value[None], (peers, *value.shape)), axis...  127 us
    all_to_all x8, waiting for transfers between devices, summed_on_arrival(): tiles = lax.all_to_all(in_blocks(value, dim, peers), axis, 0, 0, tiled=True)  95.3 us
    all_to_all x21, starting transfers between devices, copy_for_each(): lax.all_to_all(jnp.broadcast_to(value[None], (peers, *value.shape)), axis...  93.7 us
    all_gather x2, waiting for transfers between devices, sent_together(): whole, at, outs = (lax.all_gather(both, axis, axis=dim, tiled=True), 0, [])  81.1 us
    all_to_all x8, starting transfers between devices, summed_on_arrival(): tiles = lax.all_to_all(in_blocks(value, dim, peers), axis, 0, 0, tiled=True)  60 us
  transfers between devices with their start and end apart: 50, of which 38 were waited for; matrix products, arithmetic and copies ran while one was open for 19% of the time, Pallas kernels for 0%

commit v1 on v0

v1 whole, which is shorter than its diff:
```python
import functools

import jax
import jax.numpy as jnp
from jax import lax
from jax.experimental import pallas as pl
from jax.experimental.pallas import tpu as pltpu
from jax.sharding import PartitionSpec as P

D = 2048
HEAD = 128
SCALE = HEAD**-0.5
EPSILON = 1e-05
HUGE = 1e30
LOW = jnp.bfloat16
OWN = 128
VMEM_LIMIT = 56 * 2**20


def dot(a, b, contract):
    return lax.dot_general(a, b, ((contract[0], contract[1]), ((), ())), preferred_element_type=jnp.float32)


NN = ((1,), (0,))
NT = ((1,), (1,))
TN = ((0,), (0,))


def place_rows(group, half):
    row = lax.broadcasted_iota(jnp.int32, (256, 1), 0)
    return (2 * group + row // OWN) * 256 + half * OWN + row % OWN


def allowed_keys(group, extent, half, length):
    slot = lax.broadcasted_iota(jnp.int32, (256, extent), 1)
    return (slot <= place_rows(group, half)) & (slot < length)


def attend_kernel(meta_ref, q_ref, k_ref, v_ref, o_ref, lse_ref):
    half, length = meta_ref[0], meta_ref[1]
    for head in range(2):
        cols = pl.ds(head * HEAD, HEAD)
        for group in range(4):
            rows, extent = pl.ds(group * 256, 256), 512 * (group + 1)
            scores = dot(q_ref[rows, cols], k_ref[:extent, cols], NT) * SCALE
            allowed = allowed_keys(group, extent, half, length)
            scores = jnp.where(allowed, scores, -HUGE)
            highest = jnp.max(scores, -1, keepdims=True)
            weights = jnp.exp(scores - highest)
            total = jnp.sum(weights, -1, keepdims=True)
            out = dot(weights.astype(LOW), v_ref[:extent, cols], NN) / total
            o_ref[rows, cols] = out.astype(LOW)
            lse_ref[head, rows, :] = highest + jnp.log(total)


def attend(meta, q, k, v):
    vm = pl.BlockSpec(memory_space=pltpu.VMEM)
    return pl.pallas_call(
        attend_kernel,
        out_shape=(
            jax.ShapeDtypeStruct((1024, 256), LOW),
            jax.ShapeDtypeStruct((2, 1024, 1), jnp.float32),
        ),
        in_specs=[pl.BlockSpec(memory_space=pltpu.SMEM), vm, vm, vm],
        out_specs=(vm, vm),
        compiler_params=pltpu.CompilerParams(vmem_limit_bytes=VMEM_LIMIT),
        cost_estimate=pl.CostEstimate(flops=4 * 10**9, bytes_accessed=4 * 10**6, transcendentals=2 * 10**6),
    )(meta, q, k, v)


def attend_back_kernel(meta_ref, q_ref, k_ref, v_ref, do_ref, lse_ref, dq_ref, dk_ref, dv_ref):
    half, length = meta_ref[0], meta_ref[1]
    for head in range(2):
        cols = pl.ds(head * HEAD, HEAD)
        for group in reversed(range(4)):
            rows, extent = pl.ds(group * 256, 256), 512 * (group + 1)
            q, k, v, do = q_ref[rows, cols], k_ref[:extent, cols], v_ref[:extent, cols], do_ref[rows, cols]
            scores = dot(q, k, NT) * SCALE
            allowed = allowed_keys(group, extent, half, length)
            probs = jnp.exp(jnp.where(allowed, scores, -HUGE) - lse_ref[head, rows, :])
            dprobs = dot(do, v, NT)
            weighted = probs * dprobs
            delta = jnp.sum(weighted, -1, keepdims=True)
            dscores = (weighted - probs * delta).astype(LOW)
            dq_ref[rows, cols] = (dot(dscores, k, NN) * SCALE).astype(LOW)
            dk = dot(dscores, q, TN) * SCALE
            dv = dot(probs.astype(LOW), do, TN)
            if group == 3:
                dk_ref[:, cols] = dk
                dv_ref[:, cols] = dv
            else:
                dk_ref[:extent, cols] += dk
                dv_ref[:extent, cols] += dv


def attend_back(meta, q, k, v, do, lse):
    vm = pl.BlockSpec(memory_space=pltpu.VMEM)
    return pl.pallas_call(
        attend_back_kernel,
        out_shape=(
            jax.ShapeDtypeStruct((1024, 256), LOW),
            jax.ShapeDtypeStruct((2048, 256), jnp.float32),
            jax.ShapeDtypeStruct((2048, 256), jnp.float32),
        ),
        in_specs=[pl.BlockSpec(memory_space=pltpu.SMEM), vm, vm, vm, vm, vm],
        out_specs=(vm, vm, vm),
        compiler_params=pltpu.CompilerParams(vmem_limit_bytes=VMEM_LIMIT),
        cost_estimate=pl.CostEstimate(flops=10 * 10**9, bytes_accessed=8 * 10**6, transcendentals=2 * 10**6),
    )(meta, q, k, v, do, lse)


def to_own(a):
    sent = a.reshape(2, 2, 2, OWN, 256).transpose(2, 0, 1, 3, 4).reshape(8, OWN, 256)
    got = lax.all_to_all(sent, "row", 0, 0, tiled=True)
    return got.transpose(1, 0, 2).reshape(OWN, D)


def from_own(a):
    sent = a.reshape(OWN, 8, 256).transpose(1, 0, 2)
    got = lax.all_to_all(sent, "row", 0, 0, tiled=True)
    return got.reshape(2, 2, 2, OWN, 256).transpose(1, 2, 0, 3, 4).reshape(2, 2, 256, 256)


def norm(values, gain, bias):
    middle = jnp.mean(values, -1, keepdims=True)
    spread = jnp.mean(values * values, -1, keepdims=True) - middle * middle
    inverse = lax.rsqrt(spread + EPSILON)
    centred = (values - middle) * inverse
    return centred, inverse, (centred * gain + bias).astype(LOW)


def norm_back(grad, centred, inverse, gain):
    scaled = grad * gain
    return inverse * (
        scaled - jnp.mean(scaled, -1, keepdims=True) - centred * jnp.mean(scaled * centred, -1, keepdims=True)
    )


def col_gather(a):
    return lax.all_gather(a, "col", axis=0, tiled=True)


def col_reduce(a):
    return lax.psum_scatter(a.astype(LOW), "col", scatter_dimension=0, tiled=True).astype(jnp.float32)


def partner_swap(a):
    return lax.ppermute(a, "row", [(i, (i + 4) % 8) for i in range(8)])


def total_grad(a, axis):
    part = lax.psum_scatter(a.astype(LOW), "row", scatter_dimension=axis, tiled=True)
    other = lax.ppermute(part, "dp", [(0, 1), (1, 0)])
    return part.astype(jnp.float32) + other.astype(jnp.float32)


def shards(
    inputs,
    lengths,
    ln1_gain,
    ln1_bias,
    w_qkv,
    qv_bias,
    w_out,
    out_bias,
    ln2_gain,
    ln2_bias,
    w_up,
    up_bias,
    w_down,
    down_bias,
    cotangent,
):
    row = lax.axis_index("row")
    half, micro, seq = row // 4, (row // 2) % 2, row % 2
    meta = jnp.stack([half, lengths[micro, seq]]).astype(jnp.int32)
    small = jnp.stack([ln1_gain, ln1_bias, out_bias, ln2_gain, ln2_bias, down_bias])
    small = lax.all_gather(small, "row", axis=1, tiled=True)
    gain1, bias1, bias_out, gain2, bias2, bias_down = [small[i] for i in range(6)]
    wq = lax.all_gather(w_qkv, "row", axis=1, tiled=True)
    wo = lax.all_gather(w_out, "row", axis=1, tiled=True)
    wu = lax.all_gather(w_up, "row", axis=0, tiled=True)
    wd = lax.all_gather(w_down, "row", axis=1, tiled=True)

    x = to_own(inputs).astype(jnp.float32)
    dy_low = to_own(cotangent)
    dy = dy_low.astype(jnp.float32)
    centred1, inverse1, low1 = norm(x, gain1, bias1)
    all1 = col_gather(low1)
    q = (dot(all1, wq[0], NN) + qv_bias[0]).astype(LOW)
    k = dot(all1, wq[1], NN).astype(LOW)
    v = (dot(all1, wq[2], NN) + qv_bias[1]).astype(LOW)
    other = partner_swap(jnp.concatenate([k, v], 1))

    def in_place(mine, theirs):
        first = jnp.where(half == 0, mine, theirs).reshape(8, 1, OWN, 256)
        second = jnp.where(half == 0, theirs, mine).reshape(8, 1, OWN, 256)
        return jnp.concatenate([first, second], 1).reshape(2048, 256)

    k_all, v_all = in_place(k, other[:, :256]), in_place(v, other[:, 256:])
    att, lse = attend(meta, q, k_all, v_all)
    mid = x + col_reduce(dot(att, wo, NN)) + bias_out
    centred2, inverse2, low2 = norm(mid, gain2, bias2)
    all2 = col_gather(low2)
    hidden = dot(all2, wu, NN) + up_bias
    act = jax.nn.gelu(hidden, approximate=False).astype(LOW)
    second = col_reduce(dot(act, wd, NN)) + bias_down
    mixed = from_own((mid + second).astype(LOW))

    all_dy = col_gather(dy_low)
    g_down = total_grad(dot(act, all_dy, TN), 1)
    dact = dot(all_dy, wd, NT)
    _, pull = jax.vjp(lambda inner: jax.nn.gelu(inner, approximate=False), hidden)
    dhidden = pull(dact)[0].astype(LOW)
    g_up = total_grad(dot(all2, dhidden, TN), 0)
    dlow2 = col_reduce(dot(dhidden, wu, NT))
    dmid = dy + norm_back(dlow2, centred2, inverse2, gain2)
    dbranch = dmid.astype(LOW)
    all_db = col_gather(dbranch)
    g_out = total_grad(dot(att, all_db, TN), 1)
    datt = dot(all_db, wo, NT).astype(LOW)
    dq, dk, dv = attend_back(meta, q, k_all, v_all, datt, lse)
    dkv = jnp.concatenate([dk, dv], 1).reshape(8, 2, OWN, 512)
    mine = jnp.where(half == 0, dkv[:, 0], dkv[:, 1]).reshape(1024, 512)
    theirs = jnp.where(half == 0, dkv[:, 1], dkv[:, 0]).reshape(1024, 512)
    dkv = mine + partner_swap(theirs.astype(LOW)).astype(jnp.float32)
    dqkv = jnp.concatenate([dq, dkv.astype(LOW)], 1)
    g_qkv = total_grad(
        jnp.stack([dot(all1, dqkv[:, i * 256 : (i + 1) * 256], TN) for i in range(3)]), 1
    )
    dlow1 = col_reduce(
        dot(dqkv[:, :256], wq[0], NT) + dot(dqkv[:, 256:512], wq[1], NT) + dot(dqkv[:, 512:], wq[2], NT)
    )
    input_grad = from_own(dmid + norm_back(dlow1, centred1, inverse1, gain1))

    wide = jnp.stack(
        [
            jnp.sum(dlow1 * centred1, 0),
            jnp.sum(dlow1, 0),
            jnp.sum(dbranch.astype(jnp.float32), 0),
            jnp.sum(dlow2 * centred2, 0),
            jnp.sum(dlow2, 0),
            jnp.sum(dy, 0),
        ]
    )
    wide = lax.psum(wide, ("dp", "row", "col"))
    wide = lax.dynamic_slice_in_dim(wide, row * 256, 256, 1)
    lone = jnp.concatenate(
        [
            jnp.sum(dqkv[:, :256].astype(jnp.float32), 0),
            jnp.sum(dqkv[:, 512:].astype(jnp.float32), 0),
            jnp.sum(dhidden.astype(jnp.float32), 0),
        ]
    )
    lone = lax.psum(lone, ("dp", "row"))
    return (
        mixed,
        input_grad,
        wide[0],
        wide[1],
        g_qkv,
        lone[:512].reshape(2, 256),
        g_out,
        wide[2],
        wide[3],
        wide[4],
        g_up,
        lone[512:],
        g_down,
        wide[5],
    )


def solution(mesh):
    tokens = P(None, "dp", "col", "row")
    in_specs = (
        tokens,
        P(None, "dp"),
        P("row"),
        P("row"),
        P(None, "row", "col"),
        P(None, "col"),
        P("col", "row"),
        P("row"),
        P("row"),
        P("row"),
        P("row", "col"),
        P("col"),
        P("col", "row"),
        P("row"),
        tokens,
    )
    out_specs = (
        tokens,
        tokens,
        P("row"),
        P("row"),
        P(None, "row", "col"),
        P(None, "col"),
        P("col", "row"),
        P("row"),
        P("row"),
        P("row"),
        P("row", "col"),
        P("col"),
        P("col", "row"),
        P("row"),
    )
    return jax.shard_map(shards, mesh=mesh, in_specs=in_specs, out_specs=out_specs, check_vma=False)
```

time: 1770 us -> 912 us (0.52)
  waiting for transfers between devices: 967 us -> 547 us
  local copies, waits for them, and re-layouts: 166 us -> 14.8 us
  starting transfers between devices: 170 us -> 29.3 us
  matrix products: 171 us -> 97.4 us
  other arithmetic: 94.7 us -> 35.8 us
  blocking collectives: 180 us -> 145 us
  Pallas kernels: 0 us -> 23.1 us
    all_to_all x32 -> x3, waiting for transfers between devices: 308 us -> 0.01 us  [the longest x2 0.01 us: from_own(): got = lax.all_to_all(sent, 'row', 0, 0, tiled=True)]
    all_gather x12 -> x8, waiting for transfers between devices: 443 us -> 224 us  [the longest x4 122 us: col_gather(): return lax.all_gather(a, 'col', axis=0, tiled=True)]
    all_to_all x5 -> x1, blocking collectives: 180 us -> 12.2 us  [to_own(): got = lax.all_to_all(sent, 'row', 0, 0, tiled=True)]
    all_to_all x32 -> x3, starting transfers between devices: 168 us -> 15.1 us  [the longest x2 9.19 us: from_own(): got = lax.all_to_all(sent, 'row', 0, 0, tiled=True)]
    psum x0 -> x2, blocking collectives: none -> 106 us  [the longest x1 73 us: shards(): wide = lax.psum(wide, ('dp', 'row', 'col'))]
    ppermute x0 -> x6, waiting for transfers between devices: none -> 74.7 us  [the longest x2 66.8 us: partner_swap(): return lax.ppermute(a, 'row', [(i, (i + 4) % 8) for i in range(8)])]
    dot_general x36 -> x18, matrix products: 171 us -> 97.4 us  [dot(): lax.dot_general(a, b, ((contract[0], contract[1]), ((), ())), preferred_e...]
    reshape x18 -> x5, local copies, waits for them, and re-layouts: 65.6 us -> 5.71 us  [the longest x2 2.93 us: from_own(): sent = a.reshape(OWN, 8, 256).transpose(1, 0, 2)]
  transfers between devices with their start and end apart: 50 -> 25, of which waited for: 38 -> 17; matrix products, arithmetic and copies ran while one was open for 19% -> 12% of each run, Pallas kernels for 0% -> 3%
where the time goes in v1:
time: 912 us; the launch traced here: 908 us
  waiting for transfers between devices  547 us (60%)
  blocking collectives  145 us (16%)
  matrix products  97.4 us (11%)
  other arithmetic  35.8 us (4%)
  starting transfers between devices  29.3 us (3%)
  Pallas kernels  23.1 us (3%)
  local copies, waits for them, and re-layouts  14.8 us (2%)
  between operations  14.7 us (2%)
    reduce_scatter x4, waiting for transfers between devices, total_grad(): lax.psum_scatter(a.astype(LOW), 'row', scatter_dimension=axis, tiled=True)  132 us
    all_gather x4, waiting for transfers between devices, col_gather(): return lax.all_gather(a, 'col', axis=0, tiled=True)  122 us
    reduce_scatter x4, waiting for transfers between devices, col_reduce(): lax.psum_scatter(a.astype(LOW), 'col', scatter_dimension=0, tiled=True)  115 us
    dot_general x18, matrix products, dot(): lax.dot_general(a, b, ((contract[0], contract[1]), ((), ())), preferred_e...  97.4 us
    psum x1, blocking collectives, shards(): wide = lax.psum(wide, ('dp', 'row', 'col'))  73 us
    ppermute x2, waiting for transfers between devices, partner_swap(): return lax.ppermute(a, 'row', [(i, (i + 4) % 8) for i in range(8)])  66.8 us
    all_gather x1, waiting for transfers between devices, shards(): wd = lax.all_gather(w_down, 'row', axis=1, tiled=True)  49.3 us
    all_gather x1, waiting for transfers between devices, shards(): wu = lax.all_gather(w_up, 'row', axis=0, tiled=True)  42.2 us
  transfers between devices with their start and end apart: 25, of which 17 were waited for; matrix products, arithmetic and copies ran while one was open for 12% of the time, Pallas kernels for 3%

profile of v1, /device:TPU:1, one launch (start us, length us, event | category | flops | bytes accessed | tf_op | source)
XLA Modules:
  0.0 907.8 jit_solution(12931108251398591339)
XLA Ops:
  9.8 5.9 all-to-all-start
  16.6 27.4 %all_gather.27 = f32[6,2048]{1,0:T(8,128)S(1)} all-gather(f32[6,256]{1,0:T(8,128)S(1)} %stack.72), channel_id=1, replica_groups=mesh['dp'=2,'row'=8,'col'=8] {'row'}, dimensions={1}, use_global_device_ids=true | all-gather | bytes 55296 | tf_op jit(solution)/shard_map/all_gather | solution.py:178
  45.7 10.8 %all-gather.11.cloned.1.call-done = bf16[3,2048,256]{2,1,0:T(8,128)(2,1)} async-done(((bf16[3,256,256]{2,1,0:T(8,128)(2,1)}), bf16[3,2048,256]{2,1,0:T(8,128)(2,1)}) %all-gather.11.cloned.1.call-update) | async-done | bytes 3145744 | tf_op jit(solution)/shard_map/all_gather | solution.py:180
  56.5 36.4 %all-gather.9.cloned.1.call-done = bf16[1024,2048]{1,0:T(8,128)(2,1)} async-done(((bf16[128,2048]{1,0:T(8,128)(2,1)}), bf16[1024,2048]{1,0:T(8,128)(2,1)}) %all-gather.9.cloned.1.call-update) | async-done | bytes 4194320 | tf_op jit(solution)/shard_map/all_gather | solution.py:140
  108.2 22.5 %collective-permute-done = bf16[1024,512]{1,0:T(8,128)(2,1)S(1)} collective-permute-done((bf16[1024,512]{1,0:T(8,128)(2,1)}, bf16[1024,512]{1,0:T(8,128)(2,1)S(1)}, u32[]{:S(2)}, u32[]{:S(2)}) %collective-permute-start) | collective-permute-done | bytes 1048608 | tf_op jit(solution)/shard_map/ppermute | solution.py:148
  132.9 8.4 shard_map.254
  146.6 36.5 %reduce-scatter.9.cloned.1.call-done = bf16[128,2048]{1,0:T(8,128)(2,1)} async-done(((bf16[1024,2048]{1,0:T(8,128)(2,1)}), bf16[128,2048]{1,0:T(8,128)(2,1)}) %reduce-scatter.9.cloned.1.call-update) | async-done | bytes 524304 | tf_op jit(solution)/shard_map/reduce_scatter | solution.py:144
  186.5 12.2 %all_to_all.20 = bf16[8,128,256]{2,1,0:T(8,128)(2,1)S(1)} all-to-all(bf16[8,128,256]{2,1,0:T(8,128)(2,1)S(1)} %bitcast.150), channel_id=1, replica_groups=mesh['dp'=2,'row'=8,'col'=8] {'row'}, dimensions={0} | all-to-all | bytes 1048576 | tf_op jit(solution)/shard_map/all_to_all | solution.py:114
  199.8 42.2 %all-gather.17.cloned.1.call-done = bf16[2048,1024]{1,0:T(8,128)(2,1)} async-done(((bf16[256,1024]{1,0:T(8,128)(2,1)}), bf16[2048,1024]{1,0:T(8,128)(2,1)}) %all-gather.17.cloned.1.call-update) | async-done | bytes 4194320 | tf_op jit(solution)/shard_map/all_gather | solution.py:182
  242.0 32.8 %all-gather.15.cloned.1.call-done = bf16[1024,2048]{1,0:T(8,128)(2,1)} async-done(((bf16[128,2048]{1,0:T(8,128)(2,1)}), bf16[1024,2048]{1,0:T(8,128)(2,1)}) %all-gather.15.cloned.1.call-update) | async-done | bytes 4194320 | tf_op jit(solution)/shard_map/all_gather | solution.py:140
  274.8 9.9 %fusion.41 = f32[1024,1024]{1,0:T(8,128)} fusion(bf16[1024,2048]{1,0:T(8,128)(2,1)} %all-gather.15.cloned.1.call-done, bf16[2048,1024]{1,0:T(8,128)(2,1)} %all-gather.17.cloned.1.call-done), kind=kOutput, calls=%fused_computation.117 | convolution fusion | flops 4294967296 | bytes 12582912 | tf_op jit(solution)/shard_map/dot_general | solution.py:21
  284.8 49.3 %all-gather.19.cloned.1.call-done = bf16[1024,2048]{1,0:T(8,128)(2,1)} async-done(((bf16[1024,256]{1,0:T(8,128)(2,1)}), bf16[1024,2048]{1,0:T(8,128)(2,1)}) %all-gather.19.cloned.1.call-update) | async-done | bytes 4194320 | tf_op jit(solution)/shard_map/all_gather | solution.py:183
  334.1 37.2 %all-gather.21.cloned.1.call-done = bf16[1024,2048]{1,0:T(8,128)(2,1)} async-done(((bf16[128,2048]{1,0:T(8,128)(2,1)}), bf16[1024,2048]{1,0:T(8,128)(2,1)}) %all-gather.21.cloned.1.call-update) | async-done | bytes 4194320 | tf_op jit(solution)/shard_map/all_gather | solution.py:140
  371.3 18.0 %convert_reduce_fusion = (f32[1024]{0:T(1024)S(1)}, bf16[1024,1024]{1,0:T(8,128)(2,1)S(1)}, f32[1024,1024]{1,0:T(8,128)}) fusion(f32[1024,1024]{1,0:T(8,128)} %fusion.41, f32[1024]{0:T(1024)S(1)} %copy-done.12, bf16[1024,2048]{1,0:T(8,128)(2,1)} %all-gather.21.cloned.1.call-done, bf16[1024,2048]{1,0:T(8,128)(2,1)} %all-gather.19.cloned.1.call-done), kind=kOutput, calls=%fused_computation.4 | convolution fusion | flops 4373609472 | bytes 18882560 | tf_op jit(solution)/shard_map/dot_general | solution.py:21
  390.7 6.1 convolution_convert_fusion.3
  396.9 4.7 multiply_convert_fusion
  402.9 6.1 convolution_convert_fusion.4
  409.5 22.1 %reduce-scatter.13.cloned.1.call-done = bf16[128,2048]{1,0:T(8,128)(2,1)} async-done(((bf16[1024,2048]{1,0:T(8,128)(2,1)}), bf16[128,2048]{1,0:T(8,128)(2,1)}) %reduce-scatter.13.cloned.1.call-update) | async-done | bytes 524304 | tf_op jit(solution)/shard_map/reduce_scatter | solution.py:144
  433.1 37.7 %reduce-scatter.11.cloned.1.call-done = bf16[128,2048]{1,0:T(8,128)(2,1)} async-done(((bf16[1024,2048]{1,0:T(8,128)(2,1)}), bf16[128,2048]{1,0:T(8,128)(2,1)}) %reduce-scatter.11.cloned.1.call-update) | async-done | bytes 524304 | tf_op jit(solution)/shard_map/reduce_scatter | solution.py:144
  474.2 9.4 %convolution_convert_fusion.2 = bf16[2048,1024]{1,0:T(8,128)(2,1)} fusion(bf16[1024,2048]{1,0:T(8,128)(2,1)} %all-gather.15.cloned.1.call-done, bf16[1024,1024]{1,0:T(8,128)(2,1)} %copy-done.19), kind=kOutput, calls=%fused_computation.22 | convolution fusion | flops 4297064448 | bytes 10485760 | tf_op jit(solution)/shard_map/dot_general | solution.py:21
  483.6 9.7 %convolution_convert_fusion.1 = bf16[1024,2048]{1,0:T(8,128)(2,1)} fusion(bf16[1024,1024]{1,0:T(8,128)(2,1)} %copy-done.3, bf16[1024,2048]{1,0:T(8,128)(2,1)} %all-gather.21.cloned.1.call-done), kind=kOutput, calls=%fused_computation.21 | convolution fusion | flops 4297064448 | bytes 10485760 | tf_op jit(solution)/shard_map/dot_general | solution.py:21
  493.5 15.2 %all-gather.23.cloned.1.call-done = bf16[1024,2048]{1,0:T(8,128)(2,1)} async-done(((bf16[128,2048]{1,0:T(8,128)(2,1)}), bf16[1024,2048]{1,0:T(8,128)(2,1)}) %all-gather.23.cloned.1.call-update) | async-done | bytes 4194320 | tf_op jit(solution)/shard_map/all_gather | solution.py:140
  513.1 14.7 %shard_map.255 = (bf16[1024,256]{1,0:T(8,128)(2,1)}, f32[2048,256]{1,0:T(8,128)}, f32[2048,256]{1,0:T(8,128)}) custom-call(s32[2]{0:T(128)} %pad_add_fusion.meta_ref, bf16[1024,256]{1,0:T(8,128)(2,1)} %fusion.16.q_ref, bf16[2048,256]{1,0:T(8,128)(2,1)} %bitcast.154, bf16[2048,256]{1,0:T(8,128)(2,1)} %bitcast.152, ...), custom_call_target="tpu_custom_call" | custom-call | flops 10000000000 | bytes 8000000 | tf_op jit(solution)/shard_map/pallas_call | solution.py:98
  534.0 44.3 %collective-permute-done.1 = bf16[1024,512]{1,0:T(8,128)(2,1)S(1)} collective-permute-done((bf16[1024,512]{1,0:T(8,128)(2,1)S(1)}, bf16[1024,512]{1,0:T(8,128)(2,1)S(1)}, u32[]{:S(2)}, u32[]{:S(2)}) %collective-permute-start.1) | collective-permute-done | bytes 1048608 | tf_op jit(solution)/shard_map/ppermute | solution.py:148
  606.9 50.1 %reduce-scatter.23.cloned.1.call-done = bf16[1024,256]{1,0:T(8,128)(2,1)} async-done(((bf16[1024,2048]{1,0:T(8,128)(2,1)}), bf16[1024,256]{1,0:T(8,128)(2,1)}) %reduce-scatter.23.cloned.1.call-update) | async-done | bytes 524304 | tf_op jit(solution)/shard_map/reduce_scatter | solution.py:152
  664.0 7.9 collective-permute-done.5
  674.2 18.8 %reduce-scatter.15.cloned.1.call-done = bf16[128,2048]{1,0:T(8,128)(2,1)} async-done(((bf16[1024,2048]{1,0:T(8,128)(2,1)}), bf16[128,2048]{1,0:T(8,128)(2,1)}) %reduce-scatter.15.cloned.1.call-update) | async-done | bytes 524304 | tf_op jit(solution)/shard_map/reduce_scatter | solution.py:144
  697.5 5.0 all-to-all-start.3
  702.6 34.3 %reduce-scatter.19.cloned.1.call-done = bf16[256,256]{1,0:T(8,128)(2,1)} async-done(((bf16[256,2048]{1,0:T(8,128)(2,1)}), bf16[256,256]{1,0:T(8,128)(2,1)}) %reduce-scatter.19.cloned.1.call-update) | async-done | bytes 131088 | tf_op jit(solution)/shard_map/reduce_scatter | solution.py:152
  739.3 47.1 %reduce-scatter.17.cloned.1.call-done = bf16[3,256,256]{2,1,0:T(8,128)(2,1)} async-done(((bf16[3,2048,256]{2,1,0:T(8,128)(2,1)}), bf16[3,256,256]{2,1,0:T(8,128)(2,1)}) %reduce-scatter.17.cloned.1.call-update) | async-done | bytes 393232 | tf_op jit(solution)/shard_map/reduce_scatter | solution.py:152
  788.8 32.7 %psum.15 = f32[1536]{0:T(1024)S(1)} all-reduce(f32[1536]{0:T(1024)S(1)} %pad_maximum_fusion.5), channel_id=1, replica_groups=mesh['dp'=2,'row'=8,'col'=8] {'dp','row'}, use_global_device_ids=true, to_apply=%region_23.24 | all-reduce | flops 1536 | bytes 12288 | tf_op jit(solution)/shard_map/psum | solution.py:255
  826.3 73.0 %psum.14 = f32[6,2048]{1,0:T(8,128)S(1)} all-reduce(f32[6,2048]{1,0:T(8,128)S(1)} %stack.79), channel_id=1, replica_groups=mesh['dp'=2,'row'=8,'col'=8] {'dp','row','col'}, use_global_device_ids=true, to_apply=%region_18.19 | all-reduce | flops 12288 | bytes 98304 | tf_op jit(solution)/shard_map/psum | solution.py:246
  (149 shorter events, 104.6 us)
Async XLA Ops:
  7.2 49.3 %all-gather.11.cloned.1.call-start = ((), (), s32[]{:S(2)}) async-start(), calls=%async_computation.13 | async-start | bytes 3538944 | tf_op jit(solution)/shard_map/all_gather | solution.py:180
  9.8 34.3 %all-to-all-start = ((bf16[8,128,256]{2,1,0:T(8,128)(2,1)}), bf16[8,128,256]{2,1,0:T(8,128)(2,1)S(1)}, u32[]{:S(2)}, u32[]{:S(2)}) async-start(bf16[8,128,256]{2,1,0:T(8,128)(2,1)} %bitcast.2), calls=%async_computation | async-start | bytes 1048576 | tf_op jit(solution)/shard_map/all_to_all | solution.py:114
  15.7 77.1 %all-gather.9.cloned.1.call-start = ((), (), s32[]{:S(2)}) async-start(), calls=%async_computation.12 | async-start | bytes 4718592 | tf_op jit(solution)/shard_map/all_gather | solution.py:140
  44.0 52.7 %copy-start.6 = (f32[1,2048]{1,0:T(1,128)}, f32[1,2048]{1,0:T(1,128)S(1)}, u32[]{:S(2)}) copy-start(f32[1,2048]{1,0:T(1,128)S(1)} %get-tuple-element.61) | copy-start | bytes 24580
  44.5 52.2 %copy-start.8 = (f32[128]{0:T(128)}, f32[128]{0:T(128)S(1)}, u32[]{:S(2)}) copy-start(f32[128]{0:T(128)S(1)} %get-tuple-element.66) | copy-start | bytes 1540
  45.6 95.8 %all-gather.13.cloned.1.call-start = ((), (), s32[]{:S(2)}) async-start(), calls=%async_computation.14 | async-start | bytes 1179648 | tf_op jit(solution)/shard_map/all_gather | solution.py:181
  100.3 30.3 %collective-permute-start = (bf16[1024,512]{1,0:T(8,128)(2,1)}, bf16[1024,512]{1,0:T(8,128)(2,1)S(1)}, u32[]{:S(2)}, u32[]{:S(2)}) collective-permute-start(bf16[1024,512]{1,0:T(8,128)(2,1)} %pad_maximum_fusion.2), channel_id=1, source_target_pairs={{0,32},{8,40},{16,48},{24,56},{32,0},{40,8},{48,16},{56,24},{1,33}... | collective-permute-start | bytes 3145736 | tf_op jit(solution)/shard_map/ppermute | solution.py:148
  101.5 81.6 %reduce-scatter.9.cloned.1.call-start = ((), (), s32[]{:S(2)}) async-start(), calls=%async_computation.15 | async-start | bytes 4718592 | tf_op jit(solution)/shard_map/reduce_scatter | solution.py:144
  146.0 96.0 %all-gather.17.cloned.1.call-start = ((), (), s32[]{:S(2)}) async-start(), calls=%async_computation.17 | async-start | bytes 4718592 | tf_op jit(solution)/shard_map/all_gather | solution.py:182
  146.6 128.2 %all-gather.15.cloned.1.call-start = ((), (), s32[]{:S(2)}) async-start(), calls=%async_computation.16 | async-start | bytes 4718592 | tf_op jit(solution)/shard_map/all_gather | solution.py:140
  185.6 148.5 %all-gather.19.cloned.1.call-start = ((), (), s32[]{:S(2)}) async-start(), calls=%async_computation.18 | async-start | bytes 4718592 | tf_op jit(solution)/shard_map/all_gather | solution.py:183
  186.4 185.0 %all-gather.21.cloned.1.call-start = ((), (), s32[]{:S(2)}) async-start(), calls=%async_computation.20 | async-start | bytes 4718592 | tf_op jit(solution)/shard_map/all_gather | solution.py:140
  199.6 171.8 %copy-start.12 = (f32[1024]{0:T(1024)S(1)}, f32[1024]{0:T(1024)}, u32[]{:S(2)}) copy-start(f32[1024]{0:T(1024)} %param.26) | copy-start | bytes 12292
  199.6 232.1 %reduce-scatter.13.cloned.1.call-start = ((), (), s32[]{:S(2)}) async-start(), calls=%async_computation.21 | async-start | bytes 4718592 | tf_op jit(solution)/shard_map/reduce_scatter | solution.py:144
  396.8 74.0 %reduce-scatter.11.cloned.1.call-start = ((), (), s32[]{:S(2)}) async-start(), calls=%async_computation.19 | async-start | bytes 4718592 | tf_op jit(solution)/shard_map/reduce_scatter | solution.py:144
  409.0 61.8 %copy-start = (bf16[8,16,8,256]{3,2,0,1:T(8,128)(2,1)S(1)}, bf16[8,16,8,256]{3,2,0,1:T(8,128)(2,1)}, u32[]{:S(2)}) copy-start(bf16[8,16,8,256]{3,2,0,1:T(8,128)(2,1)} %copy.52) | copy-start | bytes 1572868
  409.1 99.7 %all-gather.23.cloned.1.call-start = ((), (), s32[]{:S(2)}) async-start(), calls=%async_computation.22 | async-start | bytes 4718592 | tf_op jit(solution)/shard_map/all_gather | solution.py:140
  474.1 123.9 %reduce-scatter.21.cloned.1.call-start = ((), (), s32[]{:S(2)}) async-start(), calls=%async_computation.26 | async-start | bytes 4718592 | tf_op jit(solution)/shard_map/reduce_scatter | solution.py:152
  483.5 173.5 %reduce-scatter.23.cloned.1.call-start = ((), (), s32[]{:S(2)}) async-start(), calls=%async_computation.27 | async-start | bytes 4718592 | tf_op jit(solution)/shard_map/reduce_scatter | solution.py:152
  493.3 199.7 %reduce-scatter.15.cloned.1.call-start = ((), (), s32[]{:S(2)}) async-start(), calls=%async_computation.23 | async-start | bytes 4718592 | tf_op jit(solution)/shard_map/reduce_scatter | solution.py:144
  530.9 47.4 %collective-permute-start.1 = (bf16[1024,512]{1,0:T(8,128)(2,1)S(1)}, bf16[1024,512]{1,0:T(8,128)(2,1)S(1)}, u32[]{:S(2)}, u32[]{:S(2)}) collective-permute-start(bf16[1024,512]{1,0:T(8,128)(2,1)S(1)} %bitcast.156), channel_id=1, source_target_pairs={{0,32},{8,40},{16,48},{24,56},{32,0},{40,8},{48,16},{56,24},{1,33}... | collective-permute-start | bytes 3145736 | tf_op jit(solution)/shard_map/ppermute | solution.py:148
  584.7 152.2 %reduce-scatter.19.cloned.1.call-start = ((), (), s32[]{:S(2)}) async-start(), calls=%async_computation.25 | async-start | bytes 1179648 | tf_op jit(solution)/shard_map/reduce_scatter | solution.py:152
  589.4 196.9 %reduce-scatter.17.cloned.1.call-start = ((), (), s32[]{:S(2)}) async-start(), calls=%async_computation.24 | async-start | bytes 3538944 | tf_op jit(solution)/shard_map/reduce_scatter | solution.py:152
  598.0 95.0 %copy-start.7 = (f32[1,2048]{1,0:T(1,128)S(1)}, f32[1,2048]{1,0:T(1,128)}, u32[]{:S(2)}) copy-start(f32[1,2048]{1,0:T(1,128)} %copy-done.6) | copy-start | bytes 24580
  598.0 95.0 %copy-start.9 = (f32[128]{0:T(128)S(1)}, f32[128]{0:T(128)}, u32[]{:S(2)}) copy-start(f32[128]{0:T(128)} %copy-done.8) | copy-start | bytes 1540
  598.0 95.0 %copy-start.11 = (f32[128]{0:T(128)S(1)}, f32[128]{0:T(128)}, u32[]{:S(2)}) copy-start(f32[128]{0:T(128)} %copy-done.10) | copy-start | bytes 1540
  598.0 63.6 %collective-permute-start.4 = (bf16[256,1024]{1,0:T(8,128)(2,1)}, bf16[256,1024]{1,0:T(8,128)(2,1)}, u32[]{:S(2)}, u32[]{:S(2)}) collective-permute-start(bf16[256,1024]{1,0:T(8,128)(2,1)} %reduce-scatter.21.cloned.1.call-done), channel_id=1, source_target_pairs={{0,64},{64,0},{1,65},{65,1},{2,66},{66,2},{3,67},{67,3},{4,68},{68... | collective-permute-start | bytes 1572872 | tf_op jit(solution)/shard_map/ppermute | solution.py:153
  602.7 57.1 %all-to-all-start.1 = ((bf16[8,128,256]{2,1,0:T(8,128)(2,1)}), bf16[8,128,256]{2,1,0:T(8,128)(2,1)}, u32[]{:S(2)}, u32[]{:S(2)}) async-start(bf16[8,128,256]{2,1,0:T(8,128)(2,1)} %bitcast.145), calls=%async_computation.3 | async-start | bytes 1048576 | tf_op jit(solution)/shard_map/all_to_all | solution.py:120
  657.0 14.9 %collective-permute-start.5 = (bf16[1024,256]{1,0:T(8,128)(2,1)}, bf16[1024,256]{1,0:T(8,128)(2,1)}, u32[]{:S(2)}, u32[]{:S(2)}) collective-permute-start(bf16[1024,256]{1,0:T(8,128)(2,1)} %reduce-scatter.23.cloned.1.call-done), channel_id=1, source_target_pairs={{0,64},{64,0},{1,65},{65,1},{2,66},{66,2},{3,67},{67,3},{4,68},{68... | collective-permute-start | bytes 1572872 | tf_op jit(solution)/shard_map/ppermute | solution.py:153
  697.5 202.5 %all-to-all-start.3 = ((f32[8,128,256]{2,1,0:T(8,128)}), f32[8,128,256]{2,1,0:T(8,128)S(1)}, u32[]{:S(2)}, u32[]{:S(2)}) async-start(f32[8,128,256]{2,1,0:T(8,128)} %bitcast.143), calls=%async_computation.7 | async-start | bytes 2097152 | tf_op jit(solution)/shard_map/all_to_all | solution.py:120
  736.9 85.7 %collective-permute-start.3 = (bf16[256,256]{1,0:T(8,128)(2,1)}, bf16[256,256]{1,0:T(8,128)(2,1)S(1)}, u32[]{:S(2)}, u32[]{:S(2)}) collective-permute-start(bf16[256,256]{1,0:T(8,128)(2,1)} %reduce-scatter.19.cloned.1.call-done), channel_id=1, source_target_pairs={{0,64},{64,0},{1,65},{65,1},{2,66},{66,2},{3,67},{67,3},{4,68},{68... | collective-permute-start | bytes 393224 | tf_op jit(solution)/shard_map/ppermute | solution.py:153
  786.3 38.0 %collective-permute-start.2 = (bf16[3,256,256]{2,1,0:T(8,128)(2,1)}, bf16[3,256,256]{2,1,0:T(8,128)(2,1)S(1)}, u32[]{:S(2)}, u32[]{:S(2)}) collective-permute-start(bf16[3,256,256]{2,1,0:T(8,128)(2,1)} %reduce-scatter.17.cloned.1.call-done), channel_id=1, source_target_pairs={{0,64},{64,0},{1,65},{65,1},{2,66},{66,2},{3,67},{67,3},{4,68},{68... | collective-permute-start | bytes 1179656 | tf_op jit(solution)/shard_map/ppermute | solution.py:153
  (13 other events, 191.0 us)
Sparse Core Ops, SparseCore 0:
  9.7 46.7 all-gather.10
  58.7 34.0 all-gather.8
  101.7 36.8 all-gather.12
  146.1 36.9 reduce-scatter.8
  184.7 57.3 all-gather.16
  243.6 31.2 all-gather.14
  276.4 57.6 all-gather.18
  335.8 35.4 all-gather.20
  396.9 34.6 reduce-scatter.12
  433.9 36.9 reduce-scatter.10
  474.2 34.4 all-gather.22
  511.0 74.9 reduce-scatter.20
  588.4 68.5 reduce-scatter.22
  659.3 33.6 reduce-scatter.14
  695.2 41.6 reduce-scatter.18
  739.2 47.1 reduce-scatter.16

commit v2 on v1

--- a/solution.py
+++ b/solution.py
@@ -109,6 +109,346 @@
     )(meta, q, k, v, do, lse)
 
 
+MESH = pl.DeviceIdType.MESH
+HBM = pl.BlockSpec(memory_space=pl.ANY)
+VM = pl.BlockSpec(memory_space=pltpu.VMEM)
+SM = pl.BlockSpec(memory_space=pltpu.SMEM)
+
+
+def part(start, size):
+    return pl.ds(pl.multiple_of(start, size), size)
+
+
+class Net:
+    def __init__(self, send, recv, local):
+        self.send, self.recv, self.local = send, recv, local
+        self.used, self.local_used, self.live, self.own = 0, 0, [], []
+        self.dp, self.row, self.col = (lax.axis_index(a) for a in ("dp", "row", "col"))
+        self.half, self.y = self.row // 4, self.row % 4
+        self.x = self.dp * 2 + self.half
+        self.z, self.core = self.col // 2, self.col % 2
+
+    def at(self, dx=0, dy=0, dz=0, other_core=False):
+        x, y, z = (self.x + dx) % 4, (self.y + dy) % 4, (self.z + dz) % 4
+        core = 1 - self.core if other_core else self.core
+        return {"dp": x // 2, "row": (x % 2) * 4 + y, "col": z * 2 + core}
+
+    def mate(self, shift):
+        return {"dp": self.dp, "row": (self.row + shift) % 8, "col": self.col}
+
+    def partner(self):
+        return self.mate(4)
+
+    def greet(self, more=()):
+        devices = [self.mate(d) for d in range(1, 8)]
+        devices += [{"dp": 1 - self.dp, "row": (self.row + 4) % 8, "col": self.col}]
+        devices += [self.at(dz=1), self.at(dz=3), self.at(other_core=True), *more]
+        barrier = pltpu.get_barrier_semaphore()
+        for device in devices:
+            pl.semaphore_signal(barrier, inc=1, device_id=device, device_id_type=MESH)
+        pl.semaphore_wait(barrier, len(devices))
+
+    def slots(self, count):
+        self.used += count
+        return self.used - count
+
+    def _copy(self, slot, src, dst, device):
+        return pltpu.make_async_remote_copy(
+            src_ref=src,
+            dst_ref=dst,
+            send_sem=self.send.at[slot],
+            recv_sem=self.recv.at[slot],
+            device_id=device,
+            device_id_type=MESH,
+        )
+
+    def push(self, slot, src, dst, device):
+        copy = self._copy(slot, src, dst, device)
+        copy.start()
+        self.live.append(copy)
+
+    def got(self, slot, ref):
+        self._copy(slot, ref, ref, self.at(other_core=True)).wait_recv()
+
+    def move(self, src, dst):
+        copy = pltpu.make_async_copy(src, dst, self.local.at[self.local_used])
+        self.local_used += 1
+        copy.start()
+        return copy
+
+    def store(self, src, dst):
+        self.own.append(self.move(src, dst))
+
+    def drain(self):
+        for copy in self.live:
+            copy.wait_send()
+        for copy in self.own:
+            copy.wait()
+
+
+class ColGather:
+    def __init__(self, net, buf):
+        self.net, self.buf, self.slot = net, buf, net.slots(14)
+
+    def rows(self, dz, other_core, piece):
+        net = self.net
+        core = 1 - net.core if other_core else net.core
+        return self.buf.at[part(((net.z + dz) % 4 * 2 + core) * OWN + 64 * piece, 64)]
+
+    def move(self, slot, where, piece, **to):
+        ref = self.rows(where, False, piece)
+        self.net.push(self.slot + slot, ref, ref, self.net.at(**to))
+
+    def got(self, slot, dz, piece, other_core=False):
+        self.net.got(self.slot + slot, self.rows(dz, other_core, piece))
+
+    def begin(self):
+        self.move(0, 0, 0, dz=1)
+        self.move(3, 0, 1, dz=3)
+        self.move(1, 0, 1, dz=1)
+        self.move(2, 0, 0, dz=3)
+        self.move(6, 0, 0, other_core=True)
+        self.move(7, 0, 1, other_core=True)
+
+    def hop(self):
+        self.got(0, 3, 0)
+        self.move(4, 3, 0, dz=1)
+        self.got(3, 1, 1)
+        self.move(5, 1, 1, dz=3)
+        self.move(8, 3, 0, other_core=True)
+        self.move(11, 1, 1, other_core=True)
+        self.got(1, 3, 1)
+        self.move(9, 3, 1, other_core=True)
+        self.got(2, 1, 0)
+        self.move(10, 1, 0, other_core=True)
+
+    def far(self):
+        self.got(4, 2, 0)
+        self.move(12, 2, 0, other_core=True)
+        self.got(5, 2, 1)
+        self.move(13, 2, 1, other_core=True)
+
+    def pair(self, dz):
+        slot = {0: 6, 3: 8, 1: 10, 2: 12}[dz]
+        self.got(slot, dz, 0, True)
+        self.got(slot + 1, dz, 1, True)
+
+
+class RowGather:
+    def __init__(self, net, src, buf, whole, halves):
+        self.net, self.src, self.buf, self.whole, self.halves = net, src, buf, whole, halves
+        self.slot = net.slots(11)
+
+    def place(self, dy, other=False):
+        net = self.net
+        half = 1 - net.half if other else net.half
+        return self.whole(self.buf, half * 4 + (net.y + dy) % 4)
+
+    def sideways(self, dy, src):
+        net, there = self.net, self.place(dy)
+        for side, dx in enumerate((1, 3)):
+            net.push(self.slot + 3 + dy * 2 + side, self.halves(src, side), self.halves(there, side), net.at(dx=dx))
+
+    def begin(self):
+        net, mine = self.net, self.place(0)
+        for dy in (1, 3, 2):
+            net.push(self.slot + dy - 1, self.src, mine, net.at(dy=dy))
+        self.sideways(0, self.src)
+        self.copy = net.move(self.src, mine)
+
+    def step(self, dy):
+        ref = self.place(4 - dy)
+        self.net.got(self.slot + dy - 1, ref)
+        self.sideways(4 - dy, ref)
+
+    def steps(self):
+        for dy in (1, 3, 2):
+            self.step(dy)
+
+    def finish(self):
+        self.copy.wait()
+        for dy in range(4):
+            for side in range(2):
+                self.net.got(self.slot + 3 + dy * 2 + side, self.halves(self.place(dy, True), side))
+
+
+class Swap:
+    def __init__(self, net, src_of, dst_of):
+        self.net, self.src_of, self.dst_of, self.slot = net, src_of, dst_of, net.slots(7)
+
+    def begin(self):
+        net = self.net
+        for shift in range(1, 8):
+            net.push(self.slot + shift - 1, self.src_of((net.row + shift) % 8), self.dst_of(net.row), net.mate(shift))
+        self.copy = net.move(self.src_of(net.row), self.dst_of(net.row))
+
+    def finish(self):
+        net = self.net
+        self.copy.wait()
+        for shift in range(1, 8):
+            net.got(self.slot + shift - 1, self.dst_of((net.row + 8 - shift) % 8))
+
+
+def norm_rows(values, gain, bias):
+    middle = jnp.mean(values, -1, keepdims=True)
+    spread = jnp.mean(values * values, -1, keepdims=True) - middle * middle
+    inverse = lax.rsqrt(spread + EPSILON)
+    centred = (values - middle) * inverse
+    return centred * gain + bias
+
+
+def attend_group(q, kv, head, group, half, length):
+    cols, rows, extent = pl.ds(head * HEAD, HEAD), pl.ds(group * 256, 256), 512 * (group + 1)
+    scores = dot(q[rows, cols], kv[0, :extent, cols], NT) * SCALE
+    scores = jnp.where(allowed_keys(group, extent, half, length), scores, -HUGE)
+    highest = jnp.max(scores, -1, keepdims=True)
+    weights = jnp.exp(scores - highest)
+    total = jnp.sum(weights, -1, keepdims=True)
+    out = dot(weights.astype(LOW), kv[1, :extent, cols], NN) / total
+    return out, highest + jnp.log(total)
+
+
+def first_kernel(
+    meta, inputs, cotangent, small, w_qkv, w_out, qv_bias,
+    x_out, dy_out, n1_out, q_out, kv_out, att_out, lse, wq_out, wo_out, small_out,
+    x, dy, n1, q, kv, att, wq, wo, wide, send, recv, local,
+):
+    net = Net(send, recv, local)
+    net.greet()
+    mine = part(net.col * OWN, OWN)
+
+    def token_block(ref):
+        return lambda r: ref.at[(r // 2) % 2, r % 2, part(r // 4 * OWN, OWN)]
+
+    def feature_block(ref):
+        return lambda r: ref.at[:, part(r * 256, 256)]
+
+    params = Swap(net, lambda r: small, feature_block(wide))
+    tokens = Swap(net, token_block(inputs), feature_block(x))
+    upstream = Swap(net, token_block(cotangent), lambda r: dy.at[mine, part(r * 256, 256)])
+    gather_wq = RowGather(
+        net, w_qkv, wq, lambda ref, r: ref.at[:, part(r * 256, 256)], lambda ref, h: ref.at[:, pl.ds(h * 128, 128)]
+    )
+    gather_wo = RowGather(
+        net, w_out, wo, lambda ref, r: ref.at[:, part(r * 256, 256)], lambda ref, h: ref.at[pl.ds(h * 128, 128)]
+    )
+    all_n1, all_dy = ColGather(net, n1), ColGather(net, dy)
+    keys = net.slots(8)
+
+    params.begin()
+    tokens.begin()
+    gather_wq.begin()
+    upstream.begin()
+    params.finish()
+    tokens.finish()
+    for piece in range(4):
+        rows = pl.ds(piece * 32, 32)
+        low = norm_rows(x[rows, :].astype(jnp.float32), wide[0:1, :], wide[1:2, :]).astype(LOW)
+        n1[part(net.col * OWN + piece * 32, 32), :] = low
+    all_n1.begin()
+    gather_wq.steps()
+    gather_wo.begin()
+    upstream.finish()
+    all_n1.hop()
+    all_dy.begin()
+    gather_wq.finish()
+    for dz in (0, 3, 1, 2):
+        if dz == 2:
+            all_n1.far()
+        all_n1.pair(dz)
+        block = (net.z + dz) % 4
+        rows = part(block * 256, 256)
+        values = n1[rows, :]
+        k = dot(values, wq[1], NN).astype(LOW)
+        v = (dot(values, wq[2], NN) + qv_bias[1:2, :]).astype(LOW)
+        for i in range(2):
+            there = part((block * 2 + i) * 256 + net.half * OWN, OWN)
+            kv[0, there, :] = k[i * OWN : (i + 1) * OWN]
+            kv[1, there, :] = v[i * OWN : (i + 1) * OWN]
+            ref = kv.at[:, there]
+            net.push(keys + dz * 2 + i, ref, ref, net.partner())
+        q[rows, :] = (dot(values, wq[0], NN) + qv_bias[0:1, :]).astype(LOW)
+    net.store(n1, n1_out)
+    net.store(wq, wq_out)
+    net.store(q, q_out)
+    net.store(x, x_out)
+    net.store(wide, small_out)
+    gather_wo.steps()
+    all_dy.hop()
+    for dz in (0, 3, 1, 2):
+        for i in range(2):
+            block = (net.z + dz) % 4 * 2 + i
+            net.got(keys + dz * 2 + i, kv.at[:, part(block * 256 + (1 - net.half) * OWN, OWN)])
+    net.store(kv, kv_out)
+    for head in range(2):
+        for group in range(4):
+            out, logsum = attend_group(q, kv, head, group, net.half, meta[0])
+            rows = pl.ds(group * 256, 256)
+            att[rows, pl.ds(head * HEAD, HEAD)] = out.astype(LOW)
+            lse[head, rows, :] = logsum
+        if head == 0:
+            all_dy.far()
+            gather_wo.finish()
+            net.store(wo, wo_out)
+    net.store(att, att_out)
+    for dz in range(4):
+        all_dy.pair(dz)
+    net.store(dy, dy_out)
+    net.drain()
+
+
+def low_shape(*shape):
+    return jax.ShapeDtypeStruct(shape, LOW)
+
+
+def full_shape(*shape):
+    return jax.ShapeDtypeStruct(shape, jnp.float32)
+
+
+def sems(remote, local):
+    return [
+        pltpu.SemaphoreType.DMA((remote,)),
+        pltpu.SemaphoreType.DMA((remote,)),
+        pltpu.SemaphoreType.DMA((local,)),
+    ]
+
+
+def first(meta, inputs, cotangent, small, w_qkv, w_out, qv_bias):
+    return pl.pallas_call(
+        first_kernel,
+        out_shape=(
+            low_shape(OWN, D),
+            low_shape(1024, D),
+            low_shape(1024, D),
+            low_shape(1024, 256),
+            low_shape(2, 2048, 256),
+            low_shape(1024, 256),
+            full_shape(2, 1024, 1),
+            low_shape(3, D, 256),
+            low_shape(256, D),
+            full_shape(8, D),
+        ),
+        in_specs=[SM, HBM, HBM, HBM, HBM, HBM, VM],
+        out_specs=(HBM, HBM, HBM, HBM, HBM, HBM, VM, HBM, HBM, HBM),
+        scratch_shapes=[
+            pltpu.VMEM((OWN, D), LOW),
+            pltpu.VMEM((1024, D), LOW),
+            pltpu.VMEM((1024, D), LOW),
+            pltpu.VMEM((1024, 256), LOW),
+            pltpu.VMEM((2, 2048, 256), LOW),
+            pltpu.VMEM((1024, 256), LOW),
+            pltpu.VMEM((3, D, 256), LOW),
+            pltpu.VMEM((256, D), LOW),
+            pltpu.VMEM((8, D), jnp.float32),
+            *sems(96, 24),
+        ],
+        compiler_params=pltpu.CompilerParams(
+            collective_id=1, has_side_effects=True, vmem_limit_bytes=VMEM_LIMIT
+        ),
+        cost_estimate=pl.CostEstimate(flops=40 * 10**9, bytes_accessed=30 * 10**6, transcendentals=2 * 10**6),
+    )(meta, inputs, cotangent, small, w_qkv, w_out, qv_bias)
+
+
 def to_own(a):
     sent = a.reshape(2, 2, 2, OWN, 256).transpose(2, 0, 1, 3, 4).reshape(8, OWN, 256)
     got = lax.all_to_all(sent, "row", 0, 0, tiled=True)
@@ -173,32 +513,18 @@
 ):
     row = lax.axis_index("row")
     half, micro, seq = row // 4, (row // 2) % 2, row % 2
+    length = lengths[micro, seq].reshape(1)
     meta = jnp.stack([half, lengths[micro, seq]]).astype(jnp.int32)
-    small = jnp.stack([ln1_gain, ln1_bias, out_bias, ln2_gain, ln2_bias, down_bias])
-    small = lax.all_gather(small, "row", axis=1, tiled=True)
-    gain1, bias1, bias_out, gain2, bias2, bias_down = [small[i] for i in range(6)]
-    wq = lax.all_gather(w_qkv, "row", axis=1, tiled=True)
-    wo = lax.all_gather(w_out, "row", axis=1, tiled=True)
+    zero = jnp.zeros_like(ln1_gain)
+    small = jnp.stack([ln1_gain, ln1_bias, out_bias, ln2_gain, ln2_bias, down_bias, zero, zero])
+    x, all_dy, all1, q, kv, att, lse, wq, wo, wide = first(length, inputs, cotangent, small, w_qkv, w_out, qv_bias)
+    gain1, bias1, bias_out, gain2, bias2, bias_down = [wide[i] for i in range(6)]
     wu = lax.all_gather(w_up, "row", axis=0, tiled=True)
     wd = lax.all_gather(w_down, "row", axis=1, tiled=True)
-
-    x = to_own(inputs).astype(jnp.float32)
-    dy_low = to_own(cotangent)
-    dy = dy_low.astype(jnp.float32)
-    centred1, inverse1, low1 = norm(x, gain1, bias1)
-    all1 = col_gather(low1)
-    q = (dot(all1, wq[0], NN) + qv_bias[0]).astype(LOW)
-    k = dot(all1, wq[1], NN).astype(LOW)
-    v = (dot(all1, wq[2], NN) + qv_bias[1]).astype(LOW)
-    other = partner_swap(jnp.concatenate([k, v], 1))
-
-    def in_place(mine, theirs):
-        first = jnp.where(half == 0, mine, theirs).reshape(8, 1, OWN, 256)
-        second = jnp.where(half == 0, theirs, mine).reshape(8, 1, OWN, 256)
-        return jnp.concatenate([first, second], 1).reshape(2048, 256)
-
-    k_all, v_all = in_place(k, other[:, :256]), in_place(v, other[:, 256:])
-    att, lse = attend(meta, q, k_all, v_all)
+    x = x.astype(jnp.float32)
+    dy = lax.dynamic_slice_in_dim(all_dy, lax.axis_index("col") * OWN, OWN, 0).astype(jnp.float32)
+    centred1, inverse1, _ = norm(x, gain1, bias1)
+    k_all, v_all = kv[0], kv[1]
     mid = x + col_reduce(dot(att, wo, NN)) + bias_out
     centred2, inverse2, low2 = norm(mid, gain2, bias2)
     all2 = col_gather(low2)
@@ -207,7 +533,6 @@
     second = col_reduce(dot(act, wd, NN)) + bias_down
     mixed = from_own((mid + second).astype(LOW))
 
-    all_dy = col_gather(dy_low)
     g_down = total_grad(dot(act, all_dy, TN), 1)
     dact = dot(all_dy, wd, NT)
     _, pull = jax.vjp(lambda inner: jax.nn.gelu(inner, approximate=False), hidden)

time: 912 us -> 794 us (0.87)
  waiting for transfers between devices: 547 us -> 412 us
  Pallas kernels: 23.1 us -> 93.5 us
  blocking collectives: 145 us -> 106 us
  matrix products: 97.4 us -> 86.8 us
    all_gather x4 -> x2, waiting for transfers between devices: 122 us -> 43.9 us  [col_gather(): return lax.all_gather(a, 'col', axis=0, tiled=True)]
    pallas_call x1, Pallas kernels: 8.44 us -> 78.8 us  [first(): pl.pallas_call(first_kernel, out_shape=(low_shape(OWN, D), low_shape(1024...]
    all_gather x1, waiting for transfers between devices: 42.2 us -> 14.4 us  [shards(): wu = lax.all_gather(w_up, 'row', axis=0, tiled=True)]
    all_gather x1 -> x0, blocking collectives: 27.4 us -> none  [shards(): small = lax.all_gather(small, 'row', axis=1, tiled=True)]
    ppermute x2 -> x1, waiting for transfers between devices: 66.8 us -> 44.2 us  [partner_swap(): return lax.ppermute(a, 'row', [(i, (i + 4) % 8) for i in range(8)])]
    all_to_all x1 -> x0, blocking collectives: 12.2 us -> none  [to_own(): got = lax.all_to_all(sent, 'row', 0, 0, tiled=True)]
    all_gather x2 -> x0, waiting for transfers between devices: 10.8 us -> none  [the longest x1 10.8 us: shards(): wq = lax.all_gather(w_qkv, 'row', axis=1, tiled=True)]
    dot_general x18 -> x15, matrix products: 97.4 us -> 86.8 us  [dot(): lax.dot_general(a, b, ((contract[0], contract[1]), ((), ())), preferred_e...]
  transfers between devices with their start and end apart: 25 -> 19, of which waited for: 17 -> 13; matrix products, arithmetic and copies ran while one was open for 12% -> 12% of each run, Pallas kernels for 3% -> 2%
where the time goes in v2:
time: 794 us; the launch traced here: 784 us
  waiting for transfers between devices  412 us (52%)
  blocking collectives  106 us (13%)
  Pallas kernels  93.5 us (12%)
  matrix products  86.8 us (11%)
  other arithmetic  32.3 us (4%)
  starting transfers between devices  21.2 us (3%)
  local copies, waits for them, and re-layouts  16.5 us (2%)
  between operations  16.1 us (2%)
    reduce_scatter x4, waiting for transfers between devices, total_grad(): lax.psum_scatter(a.astype(LOW), 'row', scatter_dimension=axis, tiled=True)  133 us
    reduce_scatter x4, waiting for transfers between devices, col_reduce(): lax.psum_scatter(a.astype(LOW), 'col', scatter_dimension=0, tiled=True)  120 us
    dot_general x15, matrix products, dot(): lax.dot_general(a, b, ((contract[0], contract[1]), ((), ())), preferred_e...  86.8 us
    pallas_call x1, Pallas kernels, first(): pl.pallas_call(first_kernel, out_shape=(low_shape(OWN, D), low_shape(1024...  78.8 us
    psum x1, blocking collectives, shards(): wide = lax.psum(wide, ('dp', 'row', 'col'))  73.1 us
    all_gather x1, waiting for transfers between devices, shards(): wd = lax.all_gather(w_down, 'row', axis=1, tiled=True)  47.7 us
    ppermute x1, waiting for transfers between devices, partner_swap(): return lax.ppermute(a, 'row', [(i, (i + 4) % 8) for i in range(8)])  44.2 us
    all_gather x2, waiting for transfers between devices, col_gather(): return lax.all_gather(a, 'col', axis=0, tiled=True)  43.9 us
  transfers between devices with their start and end apart: 19, of which 13 were waited for; matrix products, arithmetic and copies ran while one was open for 12% of the time, Pallas kernels for 2%

profile of v2, /device:TPU:1, one launch (start us, length us, event | category | flops | bytes accessed | tf_op | source)
XLA Modules:
  0.0 784.2 jit_solution(3297674128797328907)
XLA Ops:
  10.7 78.8 %shard_map.254 = (bf16[128,2048]{1,0:T(8,128)(2,1)}, bf16[1024,2048]{1,0:T(8,128)(2,1)}, bf16[1024,2048]{1,0:T(8,128)(2,1)}, bf16[1024,256]{1,0:T(8,128)(2,1)}, ...) custom-call(s32[1]{0:T(128)} %bitcast.meta, ...), custom_call_target="tpu_custom_call" | custom-call | flops 40000000000 | bytes 30000000 | tf_op jit(solution)/shard_map/pallas_call | solution.py:417
  89.6 4.8 convolution_convert_fusion
  95.2 36.9 %reduce-scatter.9.cloned.1.call-done = bf16[128,2048]{1,0:T(8,128)(2,1)} async-done(((bf16[1024,2048]{1,0:T(8,128)(2,1)}), bf16[128,2048]{1,0:T(8,128)(2,1)}) %reduce-scatter.9.cloned.1.call-update) | async-done | bytes 524304 | tf_op jit(solution)/shard_map/reduce_scatter | solution.py:484
  136.4 14.4 %all-gather.7.cloned.1.call-done = bf16[2048,1024]{1,0:T(8,128)(2,1)} async-done(((bf16[256,1024]{1,0:T(8,128)(2,1)}), bf16[2048,1024]{1,0:T(8,128)(2,1)}) %all-gather.7.cloned.1.call-update) | async-done | bytes 4194320 | tf_op jit(solution)/shard_map/all_gather | solution.py:522
  150.8 33.7 %all-gather.5.cloned.1.call-done = bf16[1024,2048]{1,0:T(8,128)(2,1)} async-done(((bf16[128,2048]{1,0:T(8,128)(2,1)}), bf16[1024,2048]{1,0:T(8,128)(2,1)}) %all-gather.5.cloned.1.call-update) | async-done | bytes 4194320 | tf_op jit(solution)/shard_map/all_gather | solution.py:480
  184.5 9.9 %fusion.45 = f32[1024,1024]{1,0:T(8,128)} fusion(bf16[1024,2048]{1,0:T(8,128)(2,1)} %all-gather.5.cloned.1.call-done, bf16[2048,1024]{1,0:T(8,128)(2,1)} %all-gather.7.cloned.1.call-done), kind=kOutput, calls=%fused_computation.110 | convolution fusion | flops 4294967296 | bytes 12582912 | tf_op jit(solution)/shard_map/dot_general | solution.py:21
  194.4 47.7 %all-gather.9.cloned.1.call-done = bf16[1024,2048]{1,0:T(8,128)(2,1)} async-done(((bf16[1024,256]{1,0:T(8,128)(2,1)}), bf16[1024,2048]{1,0:T(8,128)(2,1)}) %all-gather.9.cloned.1.call-update) | async-done | bytes 4194320 | tf_op jit(solution)/shard_map/all_gather | solution.py:523
  242.2 18.1 %convert_reduce_fusion = (f32[1024]{0:T(1024)S(1)}, bf16[1024,1024]{1,0:T(8,128)(2,1)S(1)}, f32[1024,1024]{1,0:T(8,128)}) fusion(f32[1024,1024]{1,0:T(8,128)} %fusion.45, f32[1024]{0:T(1024)S(1)} %copy-done.7, bf16[1024,2048]{1,0:T(8,128)(2,1)} %get-tuple-element.31, bf16[1024,2048]{1,0:T(8,128)(2,1)} %all-gather.9.cloned.1.call-done), kind=kOutput, calls=%fused_computation.4 | convolution fusion | flops 4373609472 | bytes 18882560 | tf_op jit(solution)/shard_map/dot_general | solution.py:21
  261.5 6.1 convolution_convert_fusion.3
  268.0 4.7 multiply_convert_fusion
  274.0 6.1 convolution_convert_fusion.4
  280.2 26.8 %reduce-scatter.13.cloned.1.call-done = bf16[128,2048]{1,0:T(8,128)(2,1)} async-done(((bf16[1024,2048]{1,0:T(8,128)(2,1)}), bf16[128,2048]{1,0:T(8,128)(2,1)}) %reduce-scatter.13.cloned.1.call-update) | async-done | bytes 524304 | tf_op jit(solution)/shard_map/reduce_scatter | solution.py:484
  308.9 37.7 %reduce-scatter.11.cloned.1.call-done = bf16[128,2048]{1,0:T(8,128)(2,1)} async-done(((bf16[1024,2048]{1,0:T(8,128)(2,1)}), bf16[128,2048]{1,0:T(8,128)(2,1)}) %reduce-scatter.11.cloned.1.call-update) | async-done | bytes 524304 | tf_op jit(solution)/shard_map/reduce_scatter | solution.py:484
  346.5 3.2 convert_reduce_fusion.7
  349.8 9.4 %convolution_convert_fusion.1 = bf16[1024,2048]{1,0:T(8,128)(2,1)} fusion(bf16[1024,1024]{1,0:T(8,128)(2,1)} %copy-done.4, bf16[1024,2048]{1,0:T(8,128)(2,1)} %get-tuple-element.31), kind=kOutput, calls=%fused_computation.21 | convolution fusion | flops 4297064448 | bytes 10485760 | tf_op jit(solution)/shard_map/dot_general | solution.py:21
  359.3 9.8 %convolution_convert_fusion.2 = bf16[2048,1024]{1,0:T(8,128)(2,1)} fusion(bf16[1024,2048]{1,0:T(8,128)(2,1)} %all-gather.5.cloned.1.call-done, bf16[1024,1024]{1,0:T(8,128)(2,1)} %copy-done.11), kind=kOutput, calls=%fused_computation.22 | convolution fusion | flops 4297064448 | bytes 10485760 | tf_op jit(solution)/shard_map/dot_general | solution.py:21
  373.9 10.2 %all-gather.11.cloned.1.call-done = bf16[1024,2048]{1,0:T(8,128)(2,1)} async-done(((bf16[128,2048]{1,0:T(8,128)(2,1)}), bf16[1024,2048]{1,0:T(8,128)(2,1)}) %all-gather.11.cloned.1.call-update) | async-done | bytes 4194320 | tf_op jit(solution)/shard_map/all_gather | solution.py:480
  384.2 4.3 convolution_convert_fusion.9.do_ref
  388.4 14.7 %shard_map.255 = (bf16[1024,256]{1,0:T(8,128)(2,1)}, f32[2048,256]{1,0:T(8,128)}, f32[2048,256]{1,0:T(8,128)}) custom-call(s32[2]{0:T(128)} %pad_add_fusion.meta_ref, bf16[1024,256]{1,0:T(8,128)(2,1)} %get-tuple-element.32.q_ref, bf16[2048,256]{1,0:T(8,128)(2,1)} %get-tuple-element.60.k_ref, bf16[2048,256]{1,0:T(8,128)(2,1)} %get-tuple-element.59.v_ref, ...), custom_call_target="tpu_custom_call" | custom-call | flops 10000000000 | bytes 8000000 | tf_op jit(solution)/shard_map/pallas_call | solution.py:98
  409.4 44.2 %collective-permute-done = bf16[1024,512]{1,0:T(8,128)(2,1)S(1)} collective-permute-done((bf16[1024,512]{1,0:T(8,128)(2,1)S(1)}, bf16[1024,512]{1,0:T(8,128)(2,1)S(1)}, u32[]{:S(2)}, u32[]{:S(2)}) %collective-permute-start) | collective-permute-done | bytes 1048608 | tf_op jit(solution)/shard_map/ppermute | solution.py:488
  455.3 4.7 add_convert_fusion
  460.0 4.7 convolution_convert_fusion.5
  464.8 3.7 fusion.6
  478.0 4.2 all-to-all-start
  482.2 50.2 %reduce-scatter.21.cloned.1.call-done = bf16[256,1024]{1,0:T(8,128)(2,1)} async-done(((bf16[2048,1024]{1,0:T(8,128)(2,1)}), bf16[256,1024]{1,0:T(8,128)(2,1)}) %reduce-scatter.21.cloned.1.call-update) | async-done | bytes 524304 | tf_op jit(solution)/shard_map/reduce_scatter | solution.py:492
  539.2 8.0 %collective-permute-done.3 = bf16[256,1024]{1,0:T(8,128)(2,1)} collective-permute-done((bf16[256,1024]{1,0:T(8,128)(2,1)}, bf16[256,1024]{1,0:T(8,128)(2,1)}, u32[]{:S(2)}, u32[]{:S(2)}) %collective-permute-start.3) | collective-permute-done | bytes 524320 | tf_op jit(solution)/shard_map/ppermute | solution.py:493
  549.5 18.9 %reduce-scatter.15.cloned.1.call-done = bf16[128,2048]{1,0:T(8,128)(2,1)} async-done(((bf16[1024,2048]{1,0:T(8,128)(2,1)}), bf16[128,2048]{1,0:T(8,128)(2,1)}) %reduce-scatter.15.cloned.1.call-update) | async-done | bytes 524304 | tf_op jit(solution)/shard_map/reduce_scatter | solution.py:484
  572.6 4.9 all-to-all-start.1
  577.7 34.2 %reduce-scatter.19.cloned.1.call-done = bf16[256,256]{1,0:T(8,128)(2,1)} async-done(((bf16[256,2048]{1,0:T(8,128)(2,1)}), bf16[256,256]{1,0:T(8,128)(2,1)}) %reduce-scatter.19.cloned.1.call-update) | async-done | bytes 131088 | tf_op jit(solution)/shard_map/reduce_scatter | solution.py:492
  614.2 48.2 %reduce-scatter.17.cloned.1.call-done = bf16[3,256,256]{2,1,0:T(8,128)(2,1)} async-done(((bf16[3,2048,256]{2,1,0:T(8,128)(2,1)}), bf16[3,256,256]{2,1,0:T(8,128)(2,1)}) %reduce-scatter.17.cloned.1.call-update) | async-done | bytes 393232 | tf_op jit(solution)/shard_map/reduce_scatter | solution.py:492
  664.4 32.5 %psum.15 = f32[1536]{0:T(1024)S(1)} all-reduce(f32[1536]{0:T(1024)S(1)} %pad_maximum_fusion.2), channel_id=1, replica_groups=mesh['dp'=2,'row'=8,'col'=8] {'dp','row'}, use_global_device_ids=true, to_apply=%region_23.24 | all-reduce | flops 1536 | bytes 12288 | tf_op jit(solution)/shard_map/psum | solution.py:580
  701.8 73.1 %psum.14 = f32[6,2048]{1,0:T(8,128)S(1)} all-reduce(f32[6,2048]{1,0:T(8,128)S(1)} %stack.83), channel_id=1, replica_groups=mesh['dp'=2,'row'=8,'col'=8] {'dp','row','col'}, use_global_device_ids=true, to_apply=%region_18.19 | all-reduce | flops 12288 | bytes 98304 | tf_op jit(solution)/shard_map/psum | solution.py:571
  (100 shorter events, 59.4 us)
Async XLA Ops:
  8.0 124.2 %reduce-scatter.9.cloned.1.call-start = ((), (), s32[]{:S(2)}) async-start(), calls=%async_computation.10 | async-start | bytes 4718592 | tf_op jit(solution)/shard_map/reduce_scatter | solution.py:484
  94.4 0.8 copy-start.6
  94.4 37.8 %copy-start = (bf16[128,2048]{1,0:T(8,128)(2,1)S(1)}, bf16[128,2048]{1,0:T(8,128)(2,1)}, u32[]{:S(2)}) copy-start(bf16[128,2048]{1,0:T(8,128)(2,1)} %get-tuple-element.27) | copy-start | bytes 1572868
  94.4 56.4 %all-gather.7.cloned.1.call-start = ((), (), s32[]{:S(2)}) async-start(), calls=%async_computation.12 | async-start | bytes 4718592 | tf_op jit(solution)/shard_map/all_gather | solution.py:522
  95.0 89.5 %all-gather.5.cloned.1.call-start = ((), (), s32[]{:S(2)}) async-start(), calls=%async_computation.11 | async-start | bytes 4718592 | tf_op jit(solution)/shard_map/all_gather | solution.py:480
  135.8 106.3 %all-gather.9.cloned.1.call-start = ((), (), s32[]{:S(2)}) async-start(), calls=%async_computation.13 | async-start | bytes 4718592 | tf_op jit(solution)/shard_map/all_gather | solution.py:523
  136.4 105.8 %copy-start.7 = (f32[1024]{0:T(1024)S(1)}, f32[1024]{0:T(1024)}, u32[]{:S(2)}) copy-start(f32[1024]{0:T(1024)} %param.26) | copy-start | bytes 12292
  136.4 170.6 %reduce-scatter.13.cloned.1.call-start = ((), (), s32[]{:S(2)}) async-start(), calls=%async_computation.15 | async-start | bytes 4718592 | tf_op jit(solution)/shard_map/reduce_scatter | solution.py:484
  242.2 19.4 %copy-start.8 = (bf16[2048,1024]{1,0:T(8,128)(2,1)S(1)}, bf16[2048,1024]{1,0:T(8,128)(2,1)}, u32[]{:S(2)}) copy-start(bf16[2048,1024]{1,0:T(8,128)(2,1)} %all-gather.7.cloned.1.call-done) | copy-start | bytes 12582916
  260.2 1.3 copy-start.11
  267.7 78.8 %reduce-scatter.11.cloned.1.call-start = ((), (), s32[]{:S(2)}) async-start(), calls=%async_computation.14 | async-start | bytes 4718592 | tf_op jit(solution)/shard_map/reduce_scatter | solution.py:484
  268.0 6.1 copy-start.9
  272.7 1.3 copy-start.4
  280.1 26.9 %copy-start.1 = (bf16[128,2048]{1,0:T(8,128)(2,1)S(1)}, bf16[128,2048]{1,0:T(8,128)(2,1)}, u32[]{:S(2)}) copy-start(bf16[128,2048]{1,0:T(8,128)(2,1)} %reduce-scatter.9.cloned.1.call-done) | copy-start | bytes 1572868
  280.1 104.0 %all-gather.11.cloned.1.call-start = ((), (), s32[]{:S(2)}) async-start(), calls=%async_computation.16 | async-start | bytes 4718592 | tf_op jit(solution)/shard_map/all_gather | solution.py:480
  349.8 123.6 %reduce-scatter.23.cloned.1.call-start = ((), (), s32[]{:S(2)}) async-start(), calls=%async_computation.21 | async-start | bytes 4718592 | tf_op jit(solution)/shard_map/reduce_scatter | solution.py:492
  359.2 173.2 %reduce-scatter.21.cloned.1.call-start = ((), (), s32[]{:S(2)}) async-start(), calls=%async_computation.20 | async-start | bytes 4718592 | tf_op jit(solution)/shard_map/reduce_scatter | solution.py:492
  369.1 15.1 %copy-start.5 = (bf16[256,2048]{1,0:T(8,128)(2,1)S(1)}, bf16[256,2048]{1,0:T(8,128)(2,1)}, u32[]{:S(2)}) copy-start(bf16[256,2048]{1,0:T(8,128)(2,1)} %get-tuple-element.29) | copy-start | bytes 3145732
  369.1 199.4 %reduce-scatter.15.cloned.1.call-start = ((), (), s32[]{:S(2)}) async-start(), calls=%async_computation.17 | async-start | bytes 4718592 | tf_op jit(solution)/shard_map/reduce_scatter | solution.py:484
  406.1 2.0 copy-start.2
  406.1 2.0 copy-start.3
  406.3 47.3 %collective-permute-start = (bf16[1024,512]{1,0:T(8,128)(2,1)S(1)}, bf16[1024,512]{1,0:T(8,128)(2,1)S(1)}, u32[]{:S(2)}, u32[]{:S(2)}) collective-permute-start(bf16[1024,512]{1,0:T(8,128)(2,1)S(1)} %bitcast.103), channel_id=1, source_target_pairs={{0,32},{8,40},{16,48},{24,56},{32,0},{40,8},{48,16},{56,24},{1,33}... | collective-permute-start | bytes 3145736 | tf_op jit(solution)/shard_map/ppermute | solution.py:488
  460.0 151.9 %reduce-scatter.19.cloned.1.call-start = ((), (), s32[]{:S(2)}) async-start(), calls=%async_computation.19 | async-start | bytes 1179648 | tf_op jit(solution)/shard_map/reduce_scatter | solution.py:492
  464.7 197.7 %reduce-scatter.17.cloned.1.call-start = ((), (), s32[]{:S(2)}) async-start(), calls=%async_computation.18 | async-start | bytes 3538944 | tf_op jit(solution)/shard_map/reduce_scatter | solution.py:492
  464.8 3.7 copy-start.10
  473.4 63.6 %collective-permute-start.4 = (bf16[1024,256]{1,0:T(8,128)(2,1)}, bf16[1024,256]{1,0:T(8,128)(2,1)}, u32[]{:S(2)}, u32[]{:S(2)}) collective-permute-start(bf16[1024,256]{1,0:T(8,128)(2,1)} %reduce-scatter.23.cloned.1.call-done), channel_id=1, source_target_pairs={{0,64},{64,0},{1,65},{65,1},{2,66},{66,2},{3,67},{67,3},{4,68},{68... | collective-permute-start | bytes 1572872 | tf_op jit(solution)/shard_map/ppermute | solution.py:493
  478.0 57.0 %all-to-all-start = ((bf16[8,128,256]{2,1,0:T(8,128)(2,1)}), bf16[8,128,256]{2,1,0:T(8,128)(2,1)}, u32[]{:S(2)}, u32[]{:S(2)}) async-start(bf16[8,128,256]{2,1,0:T(8,128)(2,1)} %bitcast.101), calls=%async_computation.2 | async-start | bytes 1048576 | tf_op jit(solution)/shard_map/all_to_all | solution.py:460
  532.4 14.7 %collective-permute-start.3 = (bf16[256,1024]{1,0:T(8,128)(2,1)}, bf16[256,1024]{1,0:T(8,128)(2,1)}, u32[]{:S(2)}, u32[]{:S(2)}) collective-permute-start(bf16[256,1024]{1,0:T(8,128)(2,1)} %reduce-scatter.21.cloned.1.call-done), channel_id=1, source_target_pairs={{0,64},{64,0},{1,65},{65,1},{2,66},{66,2},{3,67},{67,3},{4,68},{68... | collective-permute-start | bytes 1572872 | tf_op jit(solution)/shard_map/ppermute | solution.py:493
  572.6 203.0 %all-to-all-start.1 = ((f32[8,128,256]{2,1,0:T(8,128)}), f32[8,128,256]{2,1,0:T(8,128)S(1)}, u32[]{:S(2)}, u32[]{:S(2)}) async-start(f32[8,128,256]{2,1,0:T(8,128)} %bitcast.98), calls=%async_computation.5 | async-start | bytes 2097152 | tf_op jit(solution)/shard_map/all_to_all | solution.py:460
  611.8 86.3 %collective-permute-start.2 = (bf16[256,256]{1,0:T(8,128)(2,1)}, bf16[256,256]{1,0:T(8,128)(2,1)S(1)}, u32[]{:S(2)}, u32[]{:S(2)}) collective-permute-start(bf16[256,256]{1,0:T(8,128)(2,1)} %reduce-scatter.19.cloned.1.call-done), channel_id=1, source_target_pairs={{0,64},{64,0},{1,65},{65,1},{2,66},{66,2},{3,67},{67,3},{4,68},{68... | collective-permute-start | bytes 393224 | tf_op jit(solution)/shard_map/ppermute | solution.py:493
  662.4 37.3 %collective-permute-start.1 = (bf16[3,256,256]{2,1,0:T(8,128)(2,1)}, bf16[3,256,256]{2,1,0:T(8,128)(2,1)S(1)}, u32[]{:S(2)}, u32[]{:S(2)}) collective-permute-start(bf16[3,256,256]{2,1,0:T(8,128)(2,1)} %reduce-scatter.17.cloned.1.call-done), channel_id=1, source_target_pairs={{0,64},{64,0},{1,65},{65,1},{2,66},{66,2},{3,67},{67,3},{4,68},{68... | collective-permute-start | bytes 1179656 | tf_op jit(solution)/shard_map/ppermute | solution.py:493
Sparse Core Ops, SparseCore 0:
  94.5 37.6 reduce-scatter.8
  267.8 39.1 reduce-scatter.12
  309.4 37.0 reduce-scatter.10
Sparse Core Ops, SparseCore 1:
  96.5 54.3 all-gather.6
  153.0 31.4 all-gather.4
  186.0 56.1 all-gather.8
  349.9 34.2 all-gather.10
  386.6 74.7 reduce-scatter.22
  463.8 68.6 reduce-scatter.20
  534.7 33.7 reduce-scatter.14
  570.7 41.1 reduce-scatter.18
  614.1 48.2 reduce-scatter.16
